TPU v7x, 32 devices: a whole 2x2x4 slice. The times are simulated.
32 devices in a mesh: tile: 8 (over z, x), tm: 4 (over y, core).
Axes of the slice: x: 2, y: 2, z: 4, core: 2. Of those that a mesh axis runs over, the one named last changes fastest.
Arguments:
- volume: bfloat16 [16, 64, 16, 128], P('tm', 'tile'), may hold values from -6 to 6
- frame_index: int32 [16], P('tm'), may hold values from 0 to 31, as said below
- tile_offset: int32 [3], replicated, may hold values from 0 to 255
- conv_first: bfloat16 [16, 1, 3, 3, 3], replicated, may hold values from -1.25 to 1.25
- conv_second: bfloat16 [16, 16, 3, 3, 3], replicated, may hold values from -0.3125 to 0.3125
- patch_weight: bfloat16 [8192, 1024], replicated, may hold values from -0.5 to 0.5
- attend_weight: bfloat16 [1024, 3072], P(None, 'tile')
- mixing_weight: bfloat16 [1024, 1024], P(None, 'tile'), may hold values from -0.1875 to 0.1875
- cube_output_projector: bfloat16 [1024, 512], replicated, may hold values from -0.1875 to 0.1875
Outputs:
- prediction_tensor: bfloat16 [16, 8, 2, 16, 512], P('tm', 'tile')
Inputs may be any that keep to these rules, and one draw needn't show every extreme that they name: `frame_index`: strictly increasing; the first frame is 0 and the last is 31.
All inputs are finite; a program needn't handle non-finite values.
Results may differ from a plain program's by a relative error of at most 0.015.
Values may be sent and summed in bfloat16 or wider, within the bound.
A program may use at most 256 MiB of HBM per device.

v0:
```python
import math

import jax
import jax.numpy as jnp
from jax import lax
from jax.sharding import PartitionSpec as P

CH = 16
D = 1024
HEADS = 8
HD = 128
BLOCK_EDGE_UNITS = 8


def with_halo(cells, sides, width):
    for axis, dim in sides:
        count = lax.axis_size(axis)
        ends = count - 1
        head = lax.slice_in_dim(cells, 0, width, axis=dim)
        tail = lax.slice_in_dim(cells, cells.shape[dim] - width, cells.shape[dim], axis=dim)
        cells = jnp.concatenate(
            [
                lax.ppermute(tail, axis, [(i, (i + 1) % count) for i in range(ends)]),
                cells,
                lax.ppermute(head, axis, [((i + 1) % count, i) for i in range(ends)]),
            ],
            axis=dim,
        )
    return cells


def convolve_strip(field_in, kernel):
    return lax.conv_general_dilated(
        field_in,
        kernel,
        (1, 1, 1),
        ((0, 0), (1, 1), (1, 1)),
        dimension_numbers=("NCDHW", "OIDHW", "NCDHW"),
        preferred_element_type=jnp.float32,
    )


def settle(values_in):
    return values_in * lax.rsqrt(jnp.mean(values_in * values_in, axis=-1, keepdims=True) + 1e-05)


def embed_time(frame_index):
    frequency = jnp.exp(-math.log(1000.0) * jnp.arange(D, dtype=jnp.float32) / D)
    phase_shift = (jnp.arange(D) % 2).astype(jnp.float32) * (math.pi / 2)
    return (jnp.sin(frame_index.astype(jnp.float32)[:, None] * frequency + phase_shift), frequency)


def embed_space(tile_offset, place_x, place_z, place_y, frequency):
    along_x = (tile_offset[0] + BLOCK_EDGE_UNITS * place_x).astype(jnp.float32)
    along_z = (tile_offset[1] + BLOCK_EDGE_UNITS * place_z).astype(jnp.float32)
    along_y = (tile_offset[2] + BLOCK_EDGE_UNITS * place_y).astype(jnp.float32)
    summed = jnp.sin(along_x[:, None, None, None] * frequency) + jnp.sin(
        along_z[None, :, None, None] * frequency + 1.0
    )
    summed = summed + jnp.sin(along_y[None, None, :, None] * frequency + 2.0)
    return summed.reshape(-1, D)


def attend_frames(query, keys_all, values_all, first_frame):
    cube_count = keys_all.shape[1]
    scores = jnp.einsum(
        "tnhd,smhd->htnsm", query, keys_all, preferred_element_type=jnp.float32
    ) / math.sqrt(HD)
    scores = scores.reshape(scores.shape[0], query.shape[0], query.shape[1], -1)
    query_frame = first_frame + jnp.arange(query.shape[0])
    allowed = jnp.arange(keys_all.shape[0])[None, :] <= query_frame[:, None]
    allowed = jnp.repeat(allowed, cube_count, axis=1)
    scores = jnp.where(allowed[None, :, None, :], scores, -1e30)
    shifted = jnp.exp(scores - jnp.max(scores, axis=-1, keepdims=True))
    weights = (shifted / jnp.sum(shifted, axis=-1, keepdims=True)).astype(jnp.bfloat16)
    flat_values = values_all.reshape(-1, values_all.shape[2], values_all.shape[3])
    return jnp.einsum(
        "htnk,khd->tnhd", weights, flat_values, preferred_element_type=jnp.float32
    ).astype(jnp.bfloat16)


def local(
    volume,
    frame_index,
    tile_offset,
    conv_first,
    conv_second,
    patch_weight,
    attend_weight,
    mixing_weight,
    cube_output_projector,
):
    local_frames, width_here, cells_in_depth, height_extent = volume.shape
    tile_place = lax.axis_index("tile")
    padded = with_halo(volume, (("tile", 1),), 1)
    first_maps = jax.nn.silu(convolve_strip(padded[:, None], conv_first)).astype(jnp.bfloat16)
    first_maps = with_halo(first_maps, (("tile", 2),), 1)
    second_maps = jax.nn.silu(convolve_strip(first_maps, conv_second)).astype(jnp.bfloat16)
    stride_along_x = width_here // BLOCK_EDGE_UNITS
    patch_cubes = second_maps.reshape(
        local_frames,
        CH,
        stride_along_x,
        BLOCK_EDGE_UNITS,
        cells_in_depth // BLOCK_EDGE_UNITS,
        BLOCK_EDGE_UNITS,
        height_extent // BLOCK_EDGE_UNITS,
        BLOCK_EDGE_UNITS,
    )
    patch_cubes = patch_cubes.transpose(0, 2, 4, 6, 1, 3, 5, 7).reshape(
        -1, CH * BLOCK_EDGE_UNITS**3
    )
    encoded = jnp.dot(patch_cubes, patch_weight, preferred_element_type=jnp.float32).reshape(
        local_frames, -1, D
    )
    time_emb, frequency = embed_time(frame_index)
    place_x = tile_place * stride_along_x + jnp.arange(stride_along_x)
    space_emb = embed_space(
        tile_offset,
        place_x,
        jnp.arange(cells_in_depth // BLOCK_EDGE_UNITS),
        jnp.arange(height_extent // BLOCK_EDGE_UNITS),
        frequency,
    )
    tokens = (encoded + time_emb[:, None, :] + space_emb[None]).astype(jnp.bfloat16)
    token_rows = tokens.reshape(-1, D)
    normed = settle(token_rows.astype(jnp.float32)).astype(jnp.bfloat16)
    row_count = token_rows.shape[0]
    projected = jnp.dot(
        normed,
        lax.all_gather(attend_weight, "tile", axis=1, tiled=True),
        preferred_element_type=jnp.float32,
    ).astype(jnp.bfloat16)
    cube_count = row_count // local_frames
    projected = projected.reshape(local_frames, cube_count, 3, HEADS, HD)
    keys_values = lax.all_gather(projected[:, :, 1:], "tm", axis=0, tiled=True)
    attended = attend_frames(
        projected[:, :, 0],
        keys_values[:, :, 0],
        keys_values[:, :, 1],
        lax.axis_index("tm") * local_frames,
    )
    attended_rows = attended.reshape(row_count, D)
    mixed_terms = jnp.dot(
        attended_rows,
        lax.all_gather(mixing_weight, "tile", axis=1, tiled=True),
        preferred_element_type=jnp.float32,
    )
    residual = token_rows.astype(jnp.float32) + mixed_terms
    ending_entries = settle(residual).astype(jnp.bfloat16)
    prediction_tensor = jnp.dot(
        ending_entries, cube_output_projector, preferred_element_type=jnp.float32
    ).astype(jnp.bfloat16)
    return prediction_tensor.reshape(
        local_frames,
        stride_along_x,
        cells_in_depth // BLOCK_EDGE_UNITS,
        height_extent // BLOCK_EDGE_UNITS,
        -1,
    )


def solution(mesh):
    placed = (
        P("tm", "tile", None, None),
        P("tm"),
        P(),
        P(),
        P(),
        P(),
        P(None, "tile"),
        P(None, "tile"),
        P(),
    )
    return jax.shard_map(
        local,
        mesh=mesh,
        in_specs=placed,
        out_specs=P("tm", "tile", None, None, None),
        check_vma=False,
    )
```

profile of v0, /device:TPU:0, one launch (start us, length us, event | category | flops | bytes accessed | tf_op | source)
XLA Modules:
  0.0 506.0 jit_solution(5362938200471494051)
XLA Ops:
  7.4 4.8 collective-permute-start
  24.3 4.7 copy.19
  29.0 17.6 %multiply_convert_fusion.1 = bf16[8,16,32,17,16]{2,4,3,1,0:T(8,128)(2,1)S(1)} fusion(pred[32,17]{0,1:T(8,128)(4,1)S(1)} %copy-done.8, bf16[1,10,16,32,19]{3,0,4,2,1:T(2,128)(2,1)S(1)} %copy.19, bf16[16,1,3,3,3]{0,4,3,2,1:T(4,128)(2,1)S(1)} %copy-done.7), kind=kOutput, calls=%fused_computation.5 | convolution fusion | flops 64339968 | bytes 2424192 | tf_op jit(solution)/shard_map/conv_general_dilated | solution.py:33
  46.7 3.4 copy-done.2
  51.9 24.2 %copy.22 = bf16[8,16,32,17,16]{3,2,4,1,0:T(8,128)(2,1)} copy(bf16[8,16,32,17,16]{2,4,3,1,0:T(8,128)(2,1)} %copy-done.2) | data formatting | bytes 4456448 | tf_op jit(solution)/shard_map/convert_element_type | solution.py:96
  76.1 3.6 copy.21
  79.7 2.3 reshape.260
  83.7 4.6 collective-permute-start.2
  88.3 3.6 copy.23
  91.9 2.3 reshape.262
  96.6 21.5 %reshape.271 = bf16[8,16,4,136,16]{3,2,4,1,0:T(4,128)(2,1)} reshape(bf16[8,16,32,17,16]{3,2,4,1,0:T(8,128)(2,1)} %copy.22) | data formatting | bytes 4456448 | tf_op jit(solution)/shard_map/convert_element_type | solution.py:96
  118.1 2.6 slice_bitcast_fusion.1
  122.7 3.0 copy.42
  125.8 4.4 pad.2.clone
  130.2 24.6 %reshape.265 = bf16[16,10,16,4,8,17]{5,4,2,3,1,0:T(8,128)(2,1)} reshape(bf16[16,10,16,4,136]{4,2,3,1,0:T(8,128)(2,1)} %pad.2.clone) | data formatting | bytes 5570560 | tf_op jit(solution)/shard_map/conv_general_dilated | solution.py:33
  154.8 21.6 %slice.58 = bf16[16,10,16,4,7,2]{5,4,2,3,1,0:T(8,128)(2,1)} slice(bf16[16,10,16,4,8,17]{5,4,2,3,1,0:T(8,128)(2,1)} %reshape.265), slice={[0:16], [0:10], [0:16], [0:4], [1:8], [0:2]} | slice | bytes 573440 | tf_op jit(solution)/shard_map/conv_general_dilated | solution.py:33
  176.4 21.7 %copy_bitcast_fusion = bf16[16,10,16,32,19]{4,3,2,1,0:T(8,128)(2,1)} fusion(bf16[16,10,16,4,7,2]{5,4,2,3,1,0:T(8,128)(2,1)} %slice.58, bf16[16,10,16,4,8,17]{5,4,2,3,1,0:T(8,128)(2,1)S(1)} %copy-done.1), kind=kLoop, calls=%fused_computation.3 | loop fusion | flops 9338880 | bytes 6184960 | tf_op jit(solution)/shard_map/conv_general_dilated | solution.py:33
  198.2 28.2 %copy.26 = bf16[16,10,16,32,19]{3,0,4,2,1:T(8,128)(2,1)} copy(bf16[16,10,16,32,19]{4,3,2,1,0:T(8,128)(2,1)} %copy_bitcast_fusion) | data formatting | bytes 6225920 | tf_op jit(solution)/shard_map/conv_general_dilated | solution.py:33
  226.4 35.9 %multiply_convert_fusion = bf16[8,16,32,17,16]{2,4,3,1,0:T(8,128)(2,1)} fusion(bf16[16,10,16,32,19]{3,0,4,2,1:T(8,128)(2,1)} %copy.26, bf16[16,16,3,3,3]{1,0,4,3,2:T(8,128)(2,1)S(1)} %copy-done.6, pred[32,17]{0,1:T(8,128)(4,1)S(1)} %copy-done.8), kind=kOutput, calls=%fused_computation.4 | convolution fusion | flops 929169408 | bytes 5355552 | tf_op jit(solution)/shard_map/conv_general_dilated | solution.py:33
  262.3 24.1 %copy.27 = bf16[8,16,32,17,16]{3,2,4,1,0:T(8,128)(2,1)} copy(bf16[8,16,32,17,16]{2,4,3,1,0:T(8,128)(2,1)} %multiply_convert_fusion) | data formatting | bytes 4456448 | tf_op jit(solution)/shard_map/convert_element_type | solution.py:98
  286.4 21.3 %reshape.269 = bf16[8,16,4,136,16]{3,2,4,1,0:T(4,128)(2,1)} reshape(bf16[8,16,32,17,16]{3,2,4,1,0:T(8,128)(2,1)} %copy.27) | data formatting | bytes 4456448 | tf_op jit(solution)/shard_map/convert_element_type | solution.py:98
  307.8 2.6 slice_bitcast_fusion
  310.3 11.0 %copy.28 = bf16[4,16,8,16,128]{1,4,3,2,0:T(8,128)(2,1)} copy(bf16[4,16,8,16,128]{4,0,1,3,2:T(4,128)(2,1)S(1)} %slice_bitcast_fusion) | data formatting | bytes 4194304 | tf_op jit(solution)/shard_map/convert_element_type | solution.py:98
  321.4 51.3 %copy.29 = bf16[4,1,2,16,16,8,8,8]{3,2,7,6,5,4,0,1:T(2,128)(2,1)} copy(bf16[4,1,2,16,16,8,8,8]{4,7,3,6,2,5,0,1:T(8,128)(2,1)} %bitcast.117) | data formatting | bytes 4194304 | tf_op jit(solution)/shard_map/transpose | solution.py:110
  372.7 27.0 %dot_general.20 = bf16[4,32,8192]{1,2,0:T(8,128)(2,1)} reshape(bf16[4,1,2,16,16,8,8,8]{3,2,7,6,5,4,0,1:T(2,128)(2,1)} %copy.29) | data formatting | bytes 4194304 | tf_op jit(solution)/shard_map/dot_general | solution.py:113
  399.7 11.8 %multiply_reduce_fusion.1 = (f32[4,32]{1,0:T(4,128)S(1)}, f32[4,32,1024]{2,1,0:T(8,128)S(1)}) fusion(f32[32,1024]{1,0:T(8,128)S(1)} %bitcast.123, f32[4,1024]{1,0:T(4,128)S(1)} %copy-done.5, bf16[4,32,8192]{1,2,0:T(8,128)(2,1)} %dot_general.20, bf16[8192,1024]{1,0:T(8,128)(2,1)} %param.14), kind=kOutput, calls=%fused_computation.35 | convolution fusion | flops 2148270080 | bytes 19546624 | tf_op jit(solution)/shard_map/dot_general | solution.py:113
  411.7 3.8 fusion.7
  417.7 25.0 %all-gather.6.cloned.1.call-done = bf16[16,32,2,8,128]{4,1,0,3,2:T(8,128)(2,1)} async-done(((bf16[4,32,2,8,128]{4,1,0,3,2:T(8,128)(2,1)}), bf16[16,32,2,8,128]{4,1,0,3,2:T(8,128)(2,1)}) %all-gather.6.cloned.1.call-update) | async-done | bytes 2097168 | tf_op jit(solution)/shard_map/all_gather | solution.py:136
  442.7 6.2 %select_reduce_fusion = (f32[8,4,32]{2,1,0:T(4,128)S(1)}, f32[8,4,32,16,32]{2,4,3,1,0:T(8,128)}) fusion(pred[4,16]{1,0:T(4,128)(4,1)S(1)} %iota_compare_fusion.2, bf16[16,32,2,8,128]{4,1,0,3,2:T(8,128)(2,1)} %all-gather.6.cloned.1.call-done, bf16[4,32,1,8,128]{4,3,2,1,0:T(8,128)(2,1)S(1)} %slice.62), kind=kOutput, calls=%fused_computation.9 | convolution fusion | flops 135789568 | bytes 3412032 | tf_op jit(solution)/shard_map/tnhd,smhd->htnsm/dot_general | solution.py:66
  448.9 6.4 %copy.33 = f32[8,4,32,512]{3,2,1,0:T(8,128)} copy(f32[8,4,32,512]{2,3,1,0:T(8,128)} %bitcast.116) | data formatting | bytes 4194304 | tf_op jit(solution)/shard_map/reshape | solution.py:69
  455.3 4.5 exponential_reduce_fusion
  460.7 35.2 %all-gather.8.cloned.1.call-done = bf16[1024,1024]{1,0:T(8,128)(2,1)} async-done(((bf16[1024,128]{1,0:T(8,128)(2,1)}), bf16[1024,1024]{1,0:T(8,128)(2,1)}) %all-gather.8.cloned.1.call-update) | async-done | bytes 2097168 | tf_op jit(solution)/shard_map/all_gather | solution.py:146
  (69 shorter events, 26.5 us)
Async XLA Ops:
  6.5 491.5 %copy-start = (bf16[1024,512]{1,0:T(8,128)(2,1)S(1)}, bf16[1024,512]{1,0:T(8,128)(2,1)}, u32[]{:S(2)}) copy-start(bf16[1024,512]{1,0:T(8,128)(2,1)} %param.17) | copy-start | bytes 3145732
  6.5 405.2 %all-gather.4.cloned.1.call-start = ((), (), s32[]{:S(2)}) async-start(), calls=%async_computation | async-start | bytes 7077888 | tf_op jit(solution)/shard_map/all_gather | solution.py:131
  7.4 12.3 %collective-permute-start = (bf16[4,1,16,128]{3,2,1,0:T(8,128)(2,1)S(1)}, bf16[4,1,16,128]{3,2,1,0:T(8,128)(2,1)S(1)}, u32[]{:S(2)}, u32[]{:S(2)}) collective-permute-start(bf16[4,1,16,128]{3,2,1,0:T(8,128)(2,1)S(1)} %get-tuple-element.7), channel_id=1, source_target_pairs={{0,4},{4,8},{8,12},{12,16},{16,20},{20,24},{24,28},{1,5},{5,9},{9,... | collective-permute-start | bytes 49160 | tf_op jit(solution)/shard_map/ppermute | solution.py:23
  12.2 7.4 %collective-permute-start.1 = (bf16[4,1,16,128]{3,2,1,0:T(8,128)(2,1)S(1)}, bf16[4,1,16,128]{3,2,1,0:T(8,128)(2,1)S(1)}, u32[]{:S(2)}, u32[]{:S(2)}) collective-permute-start(bf16[4,1,16,128]{3,2,1,0:T(8,128)(2,1)S(1)} %get-tuple-element.8), channel_id=1, source_target_pairs={{4,0},{8,4},{12,8},{16,12},{20,16},{24,20},{28,24},{5,1},{9,5},{13... | collective-permute-start | bytes 49160 | tf_op jit(solution)/shard_map/ppermute | solution.py:25
  13.5 429.2 %all-gather.6.cloned.1.call-start = ((), (), s32[]{:S(2)}) async-start(), calls=%async_computation.1 | async-start | bytes 2621440 | tf_op jit(solution)/shard_map/all_gather | solution.py:136
  21.7 7.3 %copy-start.7 = (bf16[16,1,3,3,3]{0,4,3,2,1:T(4,128)(2,1)S(1)}, bf16[16,1,3,3,3]{0,4,3,2,1:T(4,128)(2,1)}, u32[]{:S(2)}) copy-start(bf16[16,1,3,3,3]{0,4,3,2,1:T(4,128)(2,1)} %param.12) | copy-start | bytes 2596
  21.7 7.3 %copy-start.8 = (pred[32,17]{0,1:T(8,128)(4,1)S(1)}, pred[32,17]{0,1:T(8,128)(4,1)}, u32[]{:S(2)}) copy-start(pred[32,17]{0,1:T(8,128)(4,1)} %constant.71) | copy-start | bytes 1636
  46.6 3.4 copy-start.2
  83.7 37.0 %collective-permute-start.2 = (bf16[4,16,1,16,128]{4,0,1,3,2:T(4,128)(2,1)}, bf16[4,16,1,16,128]{4,0,1,3,2:T(4,128)(2,1)S(1)}, u32[]{:S(2)}, u32[]{:S(2)}) collective-permute-start(bf16[4,16,1,16,128]{4,0,1,3,2:T(4,128)(2,1)} %slice_bitcast_fusion.5), channel_id=1, source_target_pairs={{0,4},{4,8},{8,12},{12,16},{16,20},{20,24},{24,28},{1,5},{5,9},{9,... | collective-permute-start | bytes 786440 | tf_op jit(solution)/shard_map/ppermute | solution.py:23
  95.3 25.4 %collective-permute-start.3 = (bf16[4,16,1,16,128]{4,0,1,3,2:T(4,128)(2,1)S(1)}, bf16[4,16,1,16,128]{4,0,1,3,2:T(4,128)(2,1)S(1)}, u32[]{:S(2)}, u32[]{:S(2)}) collective-permute-start(bf16[4,16,1,16,128]{4,0,1,3,2:T(4,128)(2,1)S(1)} %slice_bitcast_fusion.4), channel_id=1, source_target_pairs={{4,0},{8,4},{12,8},{16,12},{20,16},{24,20},{28,24},{5,1},{9,5},{13... | collective-permute-start | bytes 786440 | tf_op jit(solution)/shard_map/ppermute | solution.py:25
  154.8 21.6 %copy-start.1 = (bf16[16,10,16,4,8,17]{5,4,2,3,1,0:T(8,128)(2,1)S(1)}, bf16[16,10,16,4,8,17]{5,4,2,3,1,0:T(8,128)(2,1)}, u32[]{:S(2)}) copy-start(bf16[16,10,16,4,8,17]{5,4,2,3,1,0:T(8,128)(2,1)} %reshape.265) | copy-start | bytes 8355844
  198.2 28.3 %copy-start.6 = (bf16[16,16,3,3,3]{1,0,4,3,2:T(8,128)(2,1)S(1)}, bf16[16,16,3,3,3]{1,0,4,3,2:T(8,128)(2,1)}, u32[]{:S(2)}) copy-start(bf16[16,16,3,3,3]{1,0,4,3,2:T(8,128)(2,1)} %param.13) | copy-start | bytes 41476
  372.7 27.0 %copy-start.4 = (f32[2,16,1024]{2,1,0:T(8,128)S(1)}, f32[2,16,1024]{2,1,0:T(8,128)}, u32[]{:S(2)}) copy-start(f32[2,16,1024]{2,1,0:T(8,128)} %broadcast_add_fusion) | copy-start | bytes 393220
  372.7 27.0 %copy-start.5 = (f32[4,1024]{1,0:T(4,128)S(1)}, f32[4,1024]{1,0:T(4,128)}, u32[]{:S(2)}) copy-start(f32[4,1024]{1,0:T(4,128)} %add_sine_fusion.1) | copy-start | bytes 49156
  416.7 79.2 %all-gather.8.cloned.1.call-start = ((), (), s32[]{:S(2)}) async-start(), calls=%async_computation.2 | async-start | bytes 2359296 | tf_op jit(solution)/shard_map/all_gather | solution.py:146
  455.3 4.6 copy-start.3
  455.3 4.6 slice-start
Sparse Core Ops, SparseCore 0:
  13.7 110.7 all-gather.3
  416.8 25.8 all-gather.5
  444.8 51.0 all-gather.7
where the time goes:
time: 515 us; the launch traced here: 506 us
  local copies, waits for them, and re-layouts  304 us (59%)
  matrix products  79 us (15%)
  waiting for transfers between devices  61 us (12%)
  other arithmetic  35.4 us (7%)
  between operations  14.5 us (3%)
  starting transfers between devices  12.1 us (2%)
    conv_general_dilated x6, local copies, waits for them, and re-layouts, convolve_strip(): lax.conv_general_dilated(field_in, kernel, (1, 1, 1), ((0, 0), (1, 1), (1...  80.5 us
    convert_element_type x8, local copies, waits for them, and re-layouts, local(): jax.nn.silu(convolve_strip(padded[:, None], conv_first))  61.9 us
    convert_element_type x4, local copies, waits for them, and re-layouts, local(): jax.nn.silu(convolve_strip(first_maps, conv_second)).astype(jnp.bfloat16)  59 us
    conv_general_dilated x2, matrix products, convolve_strip(): lax.conv_general_dilated(field_in, kernel, (1, 1, 1), ((0, 0), (1, 1), (1...  53.5 us
    transpose x1, local copies, waits for them, and re-layouts, local(): patch_cubes.transpose(0, 2, 4, 6, 1, 3, 5, 7)  51.3 us
    all_gather x1, waiting for transfers between devices, local(): lax.all_gather(mixing_weight, 'tile', axis=1, tiled=True)  35.2 us
    dot_general x1, local copies, waits for them, and re-layouts, local(): jnp.dot(patch_cubes, patch_weight, preferred_element_type=jnp.float32)  27 us
    all_gather x1, waiting for transfers between devices, local(): keys_values = lax.all_gather(projected[:, :, 1:], 'tm', axis=0, tiled=True)  25 us
  transfers between devices with their start and end apart: 7, of which 2 were waited for; matrix products, arithmetic and copies ran while one was open for 80% of the time, Pallas kernels for 0%

commit v1 on v0

v1 whole, which is shorter than its diff:
```python
import functools
import math

import jax
import jax.numpy as jnp
import numpy as np
from jax import lax
from jax.experimental import pallas as pl
from jax.experimental.pallas import tpu as pltpu
from jax.sharding import PartitionSpec as P

CH = 16
D = 1024
HEADS = 8
HD = 128
EDGE = 8
TAPS = 3


def window_places():
    zin, yin = [], []
    for pair in range(3):
        zin += [2 * pair] * 8 + [2 * pair + 1] * 8
        yin += list(range(2, 10)) * 2
        zin += [2 * pair + o for o in (0, 0, 1, 1, 1, 1, 0, 0)]
        yin += [10, 11, 0, 1, 10, 11, 0, 1]
    return np.array(zin), np.array(yin)


def map_places():
    zin = [z for z in range(4) for _ in range(8)] + [z for z in range(4) for _ in range(2)]
    yin = [y + 1 for _ in range(4) for y in range(8)] + [0, 9] * 4
    return np.array(zin), np.array(yin)


def banded(row_z, row_y, col_z, col_y, taps):
    dz, dy = row_z - col_z, row_y - col_y
    total = 0.0
    for j in range(TAPS):
        for k in range(TAPS):
            total = total + jnp.where(jnp.asarray((dz == j) & (dy == k)), taps(j, k), 0.0)
    return total


def first_band(conv_first):
    group_z, group_y = map_places()
    row_z, row_y = window_places()
    col_z, col_y = np.repeat(group_z, CH), np.repeat(group_y, CH)
    taps = conv_first.reshape(CH, 27).T.astype(jnp.float32) * 0.5
    spread = jnp.tile(taps, (1, len(group_z))).reshape(3, 3, 3, 1, len(col_z))
    out = banded(row_z[:, None], row_y[:, None], col_z[None], col_y[None],
                 lambda j, k: spread[:, j, k])
    out = out.reshape(3 * len(row_z), -1)
    return jnp.pad(out, ((0, 256 - out.shape[0]), (0, 0))).astype(jnp.bfloat16)


def second_band(conv_second):
    group_z, group_y = map_places()
    col = np.arange(256)
    col_z, col_y = (col // 8) % 2, col % 8
    taps = conv_second.reshape(CH, CH, 27).transpose(2, 1, 0).astype(jnp.float32) * 0.5
    expand = jnp.asarray((col[None] // 16 == np.arange(CH)[:, None]).astype(np.float32), jnp.bfloat16)
    spread = jnp.dot(taps.reshape(-1, CH).astype(jnp.bfloat16), expand,
                     preferred_element_type=jnp.float32)
    spread = spread.reshape(3, 3, 3, 1, CH, 256)
    shape = (len(group_z), 1, 1)
    out = banded(group_z.reshape(shape), group_y.reshape(shape), col_z[None, None],
                 col_y[None, None], lambda j, k: spread[:, j, k])
    return out.reshape(3, len(group_z) * CH, 256).astype(jnp.bfloat16)


def edge_mask():
    p, zc, yc = np.arange(4), np.arange(2), np.arange(16)
    zin, side = np.arange(4), np.arange(2)
    p, _, zc, yc, zin, side, _ = np.meshgrid(
        p, np.arange(4), zc, yc, zin, side, np.arange(CH), indexing="ij")
    bad = (zin == 0) & (p == 0) & (zc == 0)
    bad |= (zin == 3) & (p == 3) & (zc == 1)
    bad |= (side == 0) & (yc == 0)
    bad |= (side == 1) & (yc == 15)
    return np.where(bad, 0.0, 1.0).reshape(512, 128)


def encode_kernel(place_ref, vol_ref, t1_ref, t2_ref, mask_ref, emb_ref, w_ref,
                  tok_ref, norm_ref, win_ref, maps_ref, acc_ref):
    step = pl.program_id(0)
    last = pl.num_programs(0) - 1

    @pl.when(step == 0)
    def _():
        acc_ref[...] = jnp.zeros_like(acc_ref)
        row = lax.broadcasted_iota(jnp.int32, (96, 128), 0) % 8
        lane = lax.broadcasted_iota(jnp.int32, (96, 128), 1)
        up_ok = (row >= 6) & (lane % 16 >= 1)
        down_ok = (row < 2) & (lane % 16 <= 14)
        zc = lax.broadcasted_iota(jnp.int32, (16, 128), 1) // 16 % 2

        @pl.loop(0, vol_ref.shape[0])
        def _(x):
            here = vol_ref[x].astype(jnp.float32)
            below = jnp.where(zc == 1, pltpu.roll(here[48:], 16, 1), 0.0)
            above = jnp.where(zc == 0, pltpu.roll(here[:16], 112, 1), 0.0)
            planes = jnp.concatenate([below, here, above], axis=0)
            halo = jnp.where(up_ok, pltpu.roll(planes, 1, 1), 0.0)
            halo = halo + jnp.where(down_ok, pltpu.roll(planes, 127, 1), 0.0)
            for q in range(6):
                win_ref[x, 24 * q:24 * q + 16] = planes[16 * q:16 * q + 16]
                win_ref[x, 24 * q + 16:24 * q + 24] = halo[16 * q:16 * q + 8] + pltpu.roll(
                    halo[16 * q + 8:16 * q + 16], 4, 0)

    slot = step % 3
    parts = []
    for p in range(4):
        rows = [win_ref[step + d, 24 * p:24 * p + 72] for d in range(3)]
        window = jnp.concatenate(rows + [jnp.zeros((40, 128), jnp.float32)], axis=0)
        parts.append(window.T.astype(jnp.bfloat16))
    window = jnp.concatenate(parts, axis=0)
    for lo, hi in ((0, 256), (256, 512), (512, 640)):
        half = jnp.dot(window, t1_ref[:, lo:hi], preferred_element_type=jnp.float32)
        maps = (half + half * jnp.tanh(half)).astype(jnp.bfloat16)
        if lo == 512:
            maps = maps * mask_ref[...]
        maps_ref[slot, :, lo:hi] = maps
    none = jnp.zeros((16, 128), jnp.bfloat16)
    for t in range(4):
        maps_ref[slot, 32 * t:32 * t + 16, 0:128] = none
        maps_ref[slot, 400 + 32 * t:416 + 32 * t, 384:512] = none

    outside = ((step == 0) & (place_ref[0] == 0)) | ((step == last) & (place_ref[0] == place_ref[1] - 1))

    @pl.when(outside)
    def _():
        maps_ref[slot] = jnp.zeros(maps_ref.shape[1:], jnp.bfloat16)

    @pl.when(step >= 2)
    def _():
        half = jnp.dot(maps_ref[(step + 1) % 3], t2_ref[0], preferred_element_type=jnp.float32)
        half += jnp.dot(maps_ref[(step + 2) % 3], t2_ref[1], preferred_element_type=jnp.float32)
        half += jnp.dot(maps_ref[slot], t2_ref[2], preferred_element_type=jnp.float32)
        second = (half + half * jnp.tanh(half)).astype(jnp.bfloat16)
        total = acc_ref[...]
        for p in range(4):
            weight = w_ref[:, 0, p].reshape(256, D)
            total += jnp.dot(second[128 * p:128 * p + 128], weight, preferred_element_type=jnp.float32)
        acc_ref[...] = total

    @pl.when(step == last)
    def _():
        tokens = (acc_ref[...] + emb_ref[...]).astype(jnp.bfloat16)
        tok_ref[...] = tokens
        wide = tokens.astype(jnp.float32)
        scale = lax.rsqrt(jnp.mean(wide * wide, axis=-1, keepdims=True) + 1e-05)
        norm_ref[...] = (wide * scale).astype(jnp.bfloat16)


def encode(place, volume_rows, t1, t2, mask, emb, patch_weight):
    planes = volume_rows.shape[0]
    whole = lambda shape: pl.BlockSpec(shape, lambda s: (0,) * len(shape))
    weight = patch_weight.reshape(CH, 8, 4, 16, D)
    return pl.pallas_call(
        encode_kernel,
        grid=(planes - 2,),
        in_specs=[
            pl.BlockSpec(memory_space=pltpu.SMEM),
            whole(volume_rows.shape), whole(t1.shape), whole(t2.shape), whole(mask.shape),
            whole(emb.shape),
            pl.BlockSpec((CH, 1, 4, 16, D), lambda s: (0, jnp.maximum(s - 2, 0), 0, 0, 0)),
        ],
        out_specs=[whole((128, D)), whole((128, D))],
        out_shape=[jax.ShapeDtypeStruct((128, D), jnp.bfloat16)] * 2,
        scratch_shapes=[
            pltpu.VMEM((planes, 144, 128), jnp.float32),
            pltpu.VMEM((3, 512, 640), jnp.bfloat16),
            pltpu.VMEM((128, D), jnp.float32),
        ],
        compiler_params=pltpu.CompilerParams(vmem_limit_bytes=40 * 2**20),
        cost_estimate=pl.CostEstimate(flops=8 * 10**9, bytes_accessed=20 * 2**20,
                                      transcendentals=5 * 10**6),
        name="encode",
    )(place, volume_rows, t1, t2, mask, emb, weight)


def settle(values_in):
    return values_in * lax.rsqrt(jnp.mean(values_in * values_in, axis=-1, keepdims=True) + 1e-05)


def embed_time(frame_index):
    frequency = jnp.exp(-math.log(1000.0) * jnp.arange(D, dtype=jnp.float32) / D)
    phase_shift = (jnp.arange(D) % 2).astype(jnp.float32) * (math.pi / 2)
    return (jnp.sin(frame_index.astype(jnp.float32)[:, None] * frequency + phase_shift), frequency)


def embed_space(tile_offset, place_x, place_z, place_y, frequency):
    along_x = (tile_offset[0] + EDGE * place_x).astype(jnp.float32)
    along_z = (tile_offset[1] + EDGE * place_z).astype(jnp.float32)
    along_y = (tile_offset[2] + EDGE * place_y).astype(jnp.float32)
    summed = jnp.sin(along_x[:, None, None, None] * frequency) + jnp.sin(
        along_z[None, :, None, None] * frequency + 1.0
    )
    summed = summed + jnp.sin(along_y[None, None, :, None] * frequency + 2.0)
    return summed.reshape(-1, D)


def attend_frames(query, keys_all, values_all, first_frame):
    cube_count = keys_all.shape[1]
    scores = jnp.einsum(
        "tnhd,smhd->htnsm", query, keys_all, preferred_element_type=jnp.float32
    ) / math.sqrt(HD)
    scores = scores.reshape(scores.shape[0], query.shape[0], query.shape[1], -1)
    query_frame = first_frame + jnp.arange(query.shape[0])
    allowed = jnp.arange(keys_all.shape[0])[None, :] <= query_frame[:, None]
    allowed = jnp.repeat(allowed, cube_count, axis=1)
    scores = jnp.where(allowed[None, :, None, :], scores, -1e30)
    shifted = jnp.exp(scores - jnp.max(scores, axis=-1, keepdims=True))
    weights = (shifted / jnp.sum(shifted, axis=-1, keepdims=True)).astype(jnp.bfloat16)
    flat_values = values_all.reshape(-1, values_all.shape[2], values_all.shape[3])
    return jnp.einsum(
        "htnk,khd->tnhd", weights, flat_values, preferred_element_type=jnp.float32
    ).astype(jnp.bfloat16)


def local(volume, frame_index, tile_offset, conv_first, conv_second, patch_weight,
          attend_weight, mixing_weight, cube_output_projector):
    frames, width, depth, height = volume.shape
    tile_place = lax.axis_index("tile")
    tiles = lax.axis_size("tile")
    rows = volume.reshape(frames, width, depth // 8, 8, height // 8, 8)
    rows = rows.transpose(1, 3, 5, 0, 2, 4).reshape(width, 64, 128)
    from_left = lax.ppermute(rows[-2:], "tile", [(i, i + 1) for i in range(tiles - 1)])
    from_right = lax.ppermute(rows[:2], "tile", [(i + 1, i) for i in range(tiles - 1)])
    volume_rows = jnp.concatenate([from_left, rows, from_right], axis=0)

    time_emb, frequency = embed_time(frame_index)
    space_emb = embed_space(tile_offset, tile_place + jnp.arange(1), jnp.arange(depth // EDGE),
                            jnp.arange(height // EDGE), frequency)
    emb = (time_emb[:, None, :] + space_emb[None]).reshape(-1, D)
    place = jnp.stack([tile_place, jnp.int32(tiles)]).astype(jnp.int32)
    token_rows, normed = encode(place, volume_rows, first_band(conv_first), second_band(conv_second),
                                jnp.asarray(edge_mask(), jnp.bfloat16), emb, patch_weight)

    row_count = token_rows.shape[0]
    projected = jnp.dot(normed, lax.all_gather(attend_weight, "tile", axis=1, tiled=True),
                        preferred_element_type=jnp.float32).astype(jnp.bfloat16)
    cube_count = row_count // frames
    projected = projected.reshape(frames, cube_count, 3, HEADS, HD)
    keys_values = lax.all_gather(projected[:, :, 1:], "tm", axis=0, tiled=True)
    attended = attend_frames(projected[:, :, 0], keys_values[:, :, 0], keys_values[:, :, 1],
                             lax.axis_index("tm") * frames)
    attended_rows = attended.reshape(row_count, D)
    mixed_terms = jnp.dot(attended_rows, lax.all_gather(mixing_weight, "tile", axis=1, tiled=True),
                          preferred_element_type=jnp.float32)
    residual = token_rows.astype(jnp.float32) + mixed_terms
    final_rows = settle(residual).astype(jnp.bfloat16)
    prediction = jnp.dot(final_rows, cube_output_projector,
                         preferred_element_type=jnp.float32).astype(jnp.bfloat16)
    return prediction.reshape(frames, width // EDGE, depth // EDGE, height // EDGE, -1)


def solution(mesh):
    placed = (P("tm", "tile", None, None), P("tm"), P(), P(), P(), P(), P(None, "tile"),
              P(None, "tile"), P())
    return jax.shard_map(local, mesh=mesh, in_specs=placed,
                         out_specs=P("tm", "tile", None, None, None), check_vma=False)
```

time: 515 us -> 203 us (0.39)
  the two profiles are of different devices: /device:TPU:0 before, /device:TPU:3 now
where the time goes in v1:
time: 203 us; the launch traced here: 200 us
  waiting for transfers between devices  108 us (53%)
  local copies, waits for them, and re-layouts  25.9 us (13%)
  Pallas kernels  20.8 us (10%)
  matrix products  14.7 us (7%)
  between operations  14.2 us (7%)
  other arithmetic  11 us (5%)
  starting transfers between devices  5.52 us (3%)
    all_gather x1, waiting for transfers between devices, local(): lax.all_gather(attend_weight, 'tile', axis=1, tiled=True)  50.7 us
    all_gather x1, waiting for transfers between devices, local(): lax.all_gather(mixing_weight, 'tile', axis=1, tiled=True)  36.2 us
    pallas_call x1, Pallas kernels, encode(): pl.pallas_call(encode_kernel, grid=(planes - 2,), in_specs=[pl.BlockSpec(...  20.8 us
    all_gather x1, waiting for transfers between devices, local(): keys_values = lax.all_gather(projected[:, :, 1:], 'tm', axis=0, tiled=True)  20.1 us
    dot_general x1, matrix products, attend_frames(): jnp.einsum('tnhd,smhd->htnsm', query, keys_all, preferred_element_type=jn...  6.2 us
    broadcast_in_dim x10, local copies, waits for them, and re-layouts, banded(): jnp.where(jnp.asarray((dz == j) & (dy == k)), taps(j, k), 0.0)  5.43 us
    reshape x1, local copies, waits for them, and re-layouts, attend_frames(): scores = scores.reshape(scores.shape[0], query.shape[0], query.shape[1], -1)  5.26 us
    reduce_sum x1, other arithmetic, attend_frames(): jnp.sum(shifted, axis=-1, keepdims=True)  4.49 us
  transfers between devices with their start and end apart: 5, of which 3 were waited for; matrix products, arithmetic and copies ran while one was open for 22% of the time, Pallas kernels for 10%

profile of v1, /device:TPU:3, one launch (start us, length us, event | category | flops | bytes accessed | tf_op | source)
XLA Modules:
  0.0 200.3 jit_solution(15854228607964335541)
XLA Ops:
  6.5 0.7 all-gather.4.cloned.1.call-update
  7.3 3.5 %reshape.347 = bf16[4,8,2,8,16,8]{5,4,3,2,1,0:T(8,128)(2,1)S(1)} reshape(bf16[4,8,16,128]{3,2,1,0:T(8,128)(2,1)} %param.29) | data formatting | bytes 262144 | tf_op jit(solution)/shard_map/reshape | solution.py:227
  10.8 1.3 fusion.26
  12.1 1.3 copy.36
  13.4 0.8 slice.88
  14.2 3.2 %collective-permute-start = (bf16[2,64,128]{2,1,0:T(8,128)(2,1)}, bf16[2,64,128]{2,1,0:T(8,128)(2,1)S(1)}, u32[]{:S(2)}, u32[]{:S(2)}) collective-permute-start(bf16[2,64,128]{2,1,0:T(8,128)(2,1)} %slice.88), channel_id=1, source_target_pairs={{0,4},{4,8},{8,12},{12,16},{16,20},{20,24},{24,28},{1,5},{5,9},{9,... | collective-permute-start | bytes 98312 | tf_op jit(solution)/shard_map/ppermute | solution.py:229
  17.4 1.3 copy.38
  18.7 0.8 slice.90
  19.5 2.1 %collective-permute-start.1 = (bf16[2,64,128]{2,1,0:T(8,128)(2,1)}, bf16[2,64,128]{2,1,0:T(8,128)(2,1)}, u32[]{:S(2)}, u32[]{:S(2)}) collective-permute-start(bf16[2,64,128]{2,1,0:T(8,128)(2,1)} %slice.90), channel_id=1, source_target_pairs={{4,0},{8,4},{12,8},{16,12},{20,16},{24,20},{28,24},{5,1},{9,5},{13... | collective-permute-start | bytes 98312 | tf_op jit(solution)/shard_map/ppermute | solution.py:230
  21.8 0.8 convert_multiply_fusion
  26.1 0.9 convolution_bitcast_fusion
  28.5 2.9 %copy.37 = bf16[8,8,8,4,2,16]{5,4,3,2,1,0:T(2,128)(2,1)S(1)} copy(bf16[8,8,8,4,2,16]{2,5,1,4,0,3:T(8,128)(2,1)} %bitcast.172) | data formatting | bytes 262144 | tf_op jit(solution)/shard_map/transpose | solution.py:228
  32.1 0.8 broadcast_in_dim.357
  32.9 0.8 broadcast_in_dim.363
  33.6 0.8 broadcast_in_dim.369
  34.4 0.8 broadcast_in_dim.375
  35.2 0.8 broadcast_in_dim.381
  35.9 0.8 broadcast_in_dim.387
  36.7 0.8 broadcast_in_dim.393
  37.6 1.6 fusion.1.t2_ref
  39.3 0.8 pad_maximum_fusion.vol_ref
  40.0 20.8 %encode.1 = (bf16[128,1024]{1,0:T(8,128)(2,1)S(1)}, bf16[128,1024]{1,0:T(8,128)(2,1)S(1)}) custom-call(s32[2]{0:T(128)S(1)} %pad_add_fusion.place_ref, bf16[12,64,128]{2,1,0:T(8,128)(2,1)S(1)} %pad_maximum_fusion.vol_ref, bf16[256,640]{1,0:T(8,128)(2,1)S(1)} %pad.5.t1_ref, bf16[3,640,256]{2,1,0:T(8,128)(2,1)S(1)} %fusion.1.t2_ref, ...), custom_call_target="tpu_custom_call" | custom-call | flops 8000000000 | bytes 20971520 | tf_op jit(solution)/shard_map/encode/pallas_call | solution.py:160
  60.9 50.7 %all-gather.4.cloned.1.call-done = bf16[1024,3072]{1,0:T(8,128)(2,1)} async-done(((bf16[1024,384]{1,0:T(8,128)(2,1)}), bf16[1024,3072]{1,0:T(8,128)(2,1)}) %all-gather.4.cloned.1.call-update) | async-done | bytes 6291472 | tf_op jit(solution)/shard_map/all_gather | solution.py:242
  111.5 3.8 %fusion.9 = bf16[16,8,24,128]{3,1,2,0:T(8,128)(2,1)S(1)} fusion(bf16[128,1024]{1,0:T(8,128)(2,1)S(1)} %get-tuple-element.8, bf16[1024,3072]{1,0:T(8,128)(2,1)} %all-gather.4.cloned.1.call-done), kind=kOutput, calls=%fused_computation.23 | convolution fusion | flops 805699584 | bytes 7340032 | tf_op jit(solution)/shard_map/dot_general | solution.py:242
  115.5 0.9 copy.58
  117.6 20.1 %all-gather.6.cloned.1.call-done = bf16[16,32,2,8,128]{4,1,0,3,2:T(8,128)(2,1)} async-done(((bf16[4,32,2,8,128]{4,1,0,3,2:T(8,128)(2,1)}), bf16[16,32,2,8,128]{4,1,0,3,2:T(8,128)(2,1)}) %all-gather.6.cloned.1.call-update) | async-done | bytes 2097168 | tf_op jit(solution)/shard_map/all_gather | solution.py:246
  137.7 6.2 %select_reduce_fusion = (f32[8,4,32]{2,1,0:T(4,128)S(1)}, f32[8,4,32,16,32]{2,4,3,1,0:T(8,128)}) fusion(pred[4,16]{1,0:T(4,128)(4,1)S(1)} %iota_compare_fusion, bf16[16,32,2,8,128]{4,1,0,3,2:T(8,128)(2,1)} %all-gather.6.cloned.1.call-done, bf16[4,32,1,8,128]{4,3,2,1,0:T(8,128)(2,1)S(1)} %slice.138), kind=kOutput, calls=%fused_computation.1 | convolution fusion | flops 135789568 | bytes 3412032 | tf_op jit(solution)/shard_map/tnhd,smhd->htnsm/dot_general | solution.py:206
  143.9 5.3 %copy.42 = f32[8,4,32,512]{3,2,1,0:T(8,128)S(1)} copy(f32[8,4,32,512]{2,3,1,0:T(8,128)} %bitcast.170) | data formatting | bytes 4194304 | tf_op jit(solution)/shard_map/reshape | solution.py:209
  149.2 4.5 %exponential_reduce_fusion = f32[8,4,32]{2,1,0:T(4,128)S(1)} fusion(f32[8,4,32,16,32]{2,4,3,1,0:T(8,128)} %get-tuple-element.33, f32[8,4,32]{2,1,0:T(4,128)S(1)} %get-tuple-element.32, pred[4,16]{1,0:T(4,128)(4,1)S(1)} %iota_compare_fusion), kind=kLoop, calls=%fused_computation | loop fusion | flops 1571840 | bytes 2105408 | tf_op jit(solution)/shard_map/reduce_sum | solution.py:215
  154.5 36.2 %all-gather.8.cloned.1.call-done = bf16[1024,1024]{1,0:T(8,128)(2,1)} async-done(((bf16[1024,128]{1,0:T(8,128)(2,1)}), bf16[1024,1024]{1,0:T(8,128)(2,1)}) %all-gather.8.cloned.1.call-update) | async-done | bytes 2097168 | tf_op jit(solution)/shard_map/all_gather | solution.py:250
  190.6 2.1 %multiply_reduce_fusion = (f32[128]{0:T(128)S(1)}, f32[128,1024]{1,0:T(8,128)S(1)}) fusion(bf16[128,1024]{1,0:T(8,128)(2,1)S(1)} %get-tuple-element.7, bf16[1024,1024]{1,0:T(8,128)(2,1)} %all-gather.8.cloned.1.call-done, bf16[16,8,8,128]{3,2,1,0:T(8,128)(2,1)S(1)} %bitcast.177), kind=kOutput, calls=%fused_computation.32 | convolution fusion | flops 268959616 | bytes 3146240 | tf_op jit(solution)/shard_map/dot_general | solution.py:250
  192.8 1.0 convolution_convert_fusion.2
  (78 shorter events, 7.2 us)
Async XLA Ops:
  6.5 186.2 %copy-start = (bf16[1024,512]{1,0:T(8,128)(2,1)S(1)}, bf16[1024,512]{1,0:T(8,128)(2,1)}, u32[]{:S(2)}) copy-start(bf16[1024,512]{1,0:T(8,128)(2,1)} %param.37) | copy-start | bytes 3145732
  6.5 105.0 %all-gather.4.cloned.1.call-start = ((), (), s32[]{:S(2)}) async-start(), calls=%async_computation | async-start | bytes 7077888 | tf_op jit(solution)/shard_map/all_gather | solution.py:242
  7.3 130.4 %all-gather.6.cloned.1.call-start = ((), (), s32[]{:S(2)}) async-start(), calls=%async_computation.1 | async-start | bytes 2621440 | tf_op jit(solution)/shard_map/all_gather | solution.py:246
  10.8 8.8 %copy-start.2 = (bf16[4,8,2,8,16,8]{5,4,3,2,1,0:T(8,128)(2,1)}, bf16[4,8,2,8,16,8]{5,4,3,2,1,0:T(8,128)(2,1)S(1)}, u32[]{:S(2)}) copy-start(bf16[4,8,2,8,16,8]{5,4,3,2,1,0:T(8,128)(2,1)S(1)} %reshape.347) | copy-start | bytes 393220
  12.1 10.8 %copy-start.15 = (s32[3]{0:T(128)S(1)}, s32[3]{0:T(128)}, u32[]{:S(2)}) copy-start(s32[3]{0:T(128)} %param.31) | copy-start | bytes 40
  12.1 13.9 %copy-start.3 = (bf16[16,16,3,3,3]{1,0,4,3,2:T(8,128)(2,1)S(1)}, bf16[16,16,3,3,3]{1,0,4,3,2:T(8,128)(2,1)}, u32[]{:S(2)}) copy-start(bf16[16,16,3,3,3]{1,0,4,3,2:T(8,128)(2,1)} %param.33) | copy-start | bytes 41476
  14.2 25.0 %collective-permute-start = (bf16[2,64,128]{2,1,0:T(8,128)(2,1)}, bf16[2,64,128]{2,1,0:T(8,128)(2,1)S(1)}, u32[]{:S(2)}, u32[]{:S(2)}) collective-permute-start(bf16[2,64,128]{2,1,0:T(8,128)(2,1)} %slice.88), channel_id=1, source_target_pairs={{0,4},{4,8},{8,12},{12,16},{16,20},{20,24},{24,28},{1,5},{5,9},{9,... | collective-permute-start | bytes 98312 | tf_op jit(solution)/shard_map/ppermute | solution.py:229
  19.5 19.7 %collective-permute-start.1 = (bf16[2,64,128]{2,1,0:T(8,128)(2,1)}, bf16[2,64,128]{2,1,0:T(8,128)(2,1)}, u32[]{:S(2)}, u32[]{:S(2)}) collective-permute-start(bf16[2,64,128]{2,1,0:T(8,128)(2,1)} %slice.90), channel_id=1, source_target_pairs={{4,0},{8,4},{12,8},{16,12},{20,16},{24,20},{28,24},{5,1},{9,5},{13... | collective-permute-start | bytes 98312 | tf_op jit(solution)/shard_map/ppermute | solution.py:230
  21.6 6.2 %copy-start.4 = (pred[72,640]{1,0:T(8,128)(4,1)S(1)}, pred[72,640]{1,0:T(8,128)(4,1)}, u32[]{:S(2)}) copy-start(pred[72,640]{1,0:T(8,128)(4,1)} %constant.106.clone) | copy-start | bytes 138244
  21.6 6.2 %copy-start.5 = (pred[72,640]{1,0:T(8,128)(4,1)S(1)}, pred[72,640]{1,0:T(8,128)(4,1)}, u32[]{:S(2)}) copy-start(pred[72,640]{1,0:T(8,128)(4,1)} %constant.107.clone) | copy-start | bytes 138244
  21.7 6.2 %copy-start.6 = (pred[72,640]{1,0:T(8,128)(4,1)S(1)}, pred[72,640]{1,0:T(8,128)(4,1)}, u32[]{:S(2)}) copy-start(pred[72,640]{1,0:T(8,128)(4,1)} %constant.108.clone) | copy-start | bytes 138244
  21.7 6.2 %copy-start.7 = (pred[72,640]{1,0:T(8,128)(4,1)S(1)}, pred[72,640]{1,0:T(8,128)(4,1)}, u32[]{:S(2)}) copy-start(pred[72,640]{1,0:T(8,128)(4,1)} %constant.109.clone) | copy-start | bytes 138244
  21.7 6.2 %copy-start.8 = (pred[72,640]{1,0:T(8,128)(4,1)S(1)}, pred[72,640]{1,0:T(8,128)(4,1)}, u32[]{:S(2)}) copy-start(pred[72,640]{1,0:T(8,128)(4,1)} %constant.110.clone) | copy-start | bytes 138244
  21.7 6.2 %copy-start.9 = (pred[72,640]{1,0:T(8,128)(4,1)S(1)}, pred[72,640]{1,0:T(8,128)(4,1)}, u32[]{:S(2)}) copy-start(pred[72,640]{1,0:T(8,128)(4,1)} %constant.111.clone) | copy-start | bytes 138244
  21.7 6.2 %copy-start.10 = (pred[72,640]{1,0:T(8,128)(4,1)S(1)}, pred[72,640]{1,0:T(8,128)(4,1)}, u32[]{:S(2)}) copy-start(pred[72,640]{1,0:T(8,128)(4,1)} %constant.112.clone) | copy-start | bytes 138244
  21.7 6.2 %copy-start.11 = (pred[72,640]{1,0:T(8,128)(4,1)S(1)}, pred[72,640]{1,0:T(8,128)(4,1)}, u32[]{:S(2)}) copy-start(pred[72,640]{1,0:T(8,128)(4,1)} %constant.113.clone) | copy-start | bytes 138244
  21.7 6.2 %copy-start.12 = (pred[72,640]{1,0:T(8,128)(4,1)S(1)}, pred[72,640]{1,0:T(8,128)(4,1)}, u32[]{:S(2)}) copy-start(pred[72,640]{1,0:T(8,128)(4,1)} %constant.114.clone) | copy-start | bytes 138244
  31.4 6.1 %copy-start.14 = (pred[40,256]{1,0:T(8,128)(4,1)S(1)}, pred[40,256]{1,0:T(8,128)(4,1)}, u32[]{:S(2)}) copy-start(pred[40,256]{1,0:T(8,128)(4,1)} %constant.136) | copy-start | bytes 30724
  31.4 6.2 %copy-start.13 = (pred[40,256]{1,0:T(8,128)(4,1)S(1)}, pred[40,256]{1,0:T(8,128)(4,1)}, u32[]{:S(2)}) copy-start(pred[40,256]{1,0:T(8,128)(4,1)} %constant.128) | copy-start | bytes 30724
  35.1 4.9 %copy-start.1 = (bf16[512,128]{1,0:T(8,128)(2,1)S(1)}, bf16[512,128]{1,0:T(8,128)(2,1)}, u32[]{:S(2)}) copy-start(bf16[512,128]{1,0:T(8,128)(2,1)} %constant.125.clone.mask_ref) | copy-start | bytes 393220
  116.5 74.1 %all-gather.8.cloned.1.call-start = ((), (), s32[]{:S(2)}) async-start(), calls=%async_computation.2 | async-start | bytes 2359296 | tf_op jit(solution)/shard_map/all_gather | solution.py:250
  149.2 4.5 %slice-start = ((bf16[16,32,2,8,128]{4,1,0,3,2:T(8,128)(2,1)}), bf16[16,32,1,8,128]{4,1,0,3,2:T(8,128)(2,1)S(1)}, s32[]{:S(2)}) async-start(bf16[16,32,2,8,128]{4,1,0,3,2:T(8,128)(2,1)} %all-gather.6.cloned.1.call-done), calls=%async_computation.3 | async-start | bytes 2097152 | tf_op jit(solution)/shard_map/slice | solution.py:247
Sparse Core Ops, SparseCore 0:
  9.4 102.0 all-gather.3
  116.6 21.0 all-gather.5
  139.7 50.8 all-gather.7

commit v2 on v1

--- a/solution.py
+++ b/solution.py
@@ -35,10 +35,12 @@
 
 def banded(row_z, row_y, col_z, col_y, taps):
     dz, dy = row_z - col_z, row_y - col_y
+    shared = (dz >= 0) & (dz < TAPS) & (dy >= 0) & (dy < TAPS)
+    code = jnp.asarray(np.where(shared, dz * TAPS + dy, -1).astype(np.float32))
     total = 0.0
     for j in range(TAPS):
         for k in range(TAPS):
-            total = total + jnp.where(jnp.asarray((dz == j) & (dy == k)), taps(j, k), 0.0)
+            total = total + jnp.where(code == float(j * TAPS + k), taps(j, k), 0.0)
     return total
 
 
@@ -201,22 +203,114 @@
     return summed.reshape(-1, D)
 
 
-def attend_frames(query, keys_all, values_all, first_frame):
-    cube_count = keys_all.shape[1]
-    scores = jnp.einsum(
-        "tnhd,smhd->htnsm", query, keys_all, preferred_element_type=jnp.float32
-    ) / math.sqrt(HD)
-    scores = scores.reshape(scores.shape[0], query.shape[0], query.shape[1], -1)
-    query_frame = first_frame + jnp.arange(query.shape[0])
-    allowed = jnp.arange(keys_all.shape[0])[None, :] <= query_frame[:, None]
-    allowed = jnp.repeat(allowed, cube_count, axis=1)
-    scores = jnp.where(allowed[None, :, None, :], scores, -1e30)
-    shifted = jnp.exp(scores - jnp.max(scores, axis=-1, keepdims=True))
-    weights = (shifted / jnp.sum(shifted, axis=-1, keepdims=True)).astype(jnp.bfloat16)
-    flat_values = values_all.reshape(-1, values_all.shape[2], values_all.shape[3])
-    return jnp.einsum(
-        "htnk,khd->tnhd", weights, flat_values, preferred_element_type=jnp.float32
-    ).astype(jnp.bfloat16)
+def partners():
+    me = lax.axis_index("tm")
+    sibling = me + 1 - 2 * (me % 2)
+    return me, (sibling, (me + 2) % 4, (sibling + 2) % 4)
+
+
+def attend_kernel(norm_ref, w0_ref, w1_ref, w2_ref, w3_ref, out_ref, rows_ref, qkv_ref, att_ref,
+                  back_ref, send_sem, recv_sem, send_back, recv_back):
+    me, others = partners()
+    barrier = pltpu.get_barrier_semaphore()
+    for other in others:
+        pl.semaphore_signal(barrier, inc=1, device_id={"tm": other},
+                            device_id_type=pl.DeviceIdType.MESH)
+    pl.semaphore_wait(barrier, 3)
+    sends = [
+        pltpu.make_async_remote_copy(
+            src_ref=norm_ref, dst_ref=rows_ref.at[me], send_sem=send_sem.at[i],
+            recv_sem=recv_sem.at[i], device_id={"tm": other},
+            device_id_type=pl.DeviceIdType.MESH)
+        for i, other in enumerate(others)
+    ]
+    for send in sends:
+        send.start()
+
+    def project(block, source):
+        total = jnp.zeros((128, 768), jnp.float32)
+        for owner, w_ref in zip((me,) + others, (w0_ref, w1_ref, w2_ref, w3_ref)):
+            part = source[:, pl.ds(pl.multiple_of(owner * 256, 256), 256)]
+            total += jnp.dot(part, w_ref[...], preferred_element_type=jnp.float32)
+        qkv_ref[block] = total.astype(jnp.bfloat16)
+
+    project(me, norm_ref)
+    for i, other in enumerate(others):
+        sends[i].wait_recv()
+        project(other, rows_ref.at[other])
+
+    for head in range(2):
+        lo = head * HD
+        for block in range(4):
+            query = qkv_ref[block, :, lo:lo + HD]
+            count = 128 * (block + 1)
+            keys = qkv_ref[:block + 1, :, 256 + lo:256 + lo + HD].reshape(count, HD)
+            values = qkv_ref[:block + 1, :, 512 + lo:512 + lo + HD].reshape(count, HD)
+            scores = lax.dot_general(query, keys, (((1,), (1,)), ((), ())),
+                                     preferred_element_type=jnp.float32) / math.sqrt(HD)
+            row = lax.broadcasted_iota(jnp.int32, (128, count), 0) // 32
+            col = lax.broadcasted_iota(jnp.int32, (128, count), 1) // 32
+            scores = jnp.where(col <= row + 4 * block, scores, -1e30)
+            shifted = jnp.exp(scores - jnp.max(scores, axis=-1, keepdims=True))
+            inverse = 1.0 / jnp.sum(shifted, axis=-1, keepdims=True)
+            weights = (shifted * inverse).astype(jnp.bfloat16)
+            att_ref[block, :, lo:lo + HD] = jnp.dot(
+                weights, values, preferred_element_type=jnp.float32).astype(jnp.bfloat16)
+
+    backs = [
+        pltpu.make_async_remote_copy(
+            src_ref=att_ref.at[other], dst_ref=back_ref.at[me], send_sem=send_back.at[i],
+            recv_sem=recv_back.at[i], device_id={"tm": other},
+            device_id_type=pl.DeviceIdType.MESH)
+        for i, other in enumerate(others)
+    ]
+    for back in backs:
+        back.start()
+    out_ref[:, pl.ds(pl.multiple_of(me * 256, 256), 256)] = att_ref[me]
+    for i, other in enumerate(others):
+        backs[i].wait_recv()
+        out_ref[:, pl.ds(pl.multiple_of(other * 256, 256), 256)] = back_ref[other]
+    for i in range(3):
+        sends[i].wait_send()
+        backs[i].wait_send()
+
+
+def attend(normed, weights):
+    vmem = pl.BlockSpec(memory_space=pltpu.VMEM)
+    return pl.pallas_call(
+        attend_kernel,
+        in_specs=[vmem] * 5,
+        out_specs=vmem,
+        out_shape=jax.ShapeDtypeStruct((128, D), jnp.bfloat16),
+        scratch_shapes=[
+            pltpu.VMEM((4, 128, D), jnp.bfloat16),
+            pltpu.VMEM((4, 128, 768), jnp.bfloat16),
+            pltpu.VMEM((4, 128, 256), jnp.bfloat16),
+            pltpu.VMEM((4, 128, 256), jnp.bfloat16),
+        ] + [pltpu.SemaphoreType.DMA((3,))] * 4,
+        compiler_params=pltpu.CompilerParams(collective_id=0, has_side_effects=True,
+                                             vmem_limit_bytes=32 * 2**20),
+        cost_estimate=pl.CostEstimate(flops=10**9, bytes_accessed=2 * 2**20,
+                                      transcendentals=4 * 10**5),
+        name="attend",
+    )(normed, *weights)
+
+
+def head_weights(attend_weight):
+    me = lax.axis_index("tm")
+    quarter = lax.dynamic_slice_in_dim(attend_weight, me * 256, 256, axis=0)
+    quarter = lax.all_gather(quarter, "tile", axis=1, tiled=True)
+
+    def columns(member):
+        return jnp.concatenate(
+            [lax.dynamic_slice_in_dim(quarter, j * D + member * 256, 256, axis=1) for j in range(3)],
+            axis=1)
+
+    me, others = partners()
+    pieces = [columns(me)]
+    for i, other in enumerate(others):
+        pieces.append(lax.ppermute(columns(other), "tm", [(m, m ^ (i + 1)) for m in range(4)]))
+    return pieces
 
 
 def local(volume, frame_index, tile_offset, conv_first, conv_second, patch_weight,
@@ -238,15 +332,7 @@
     token_rows, normed = encode(place, volume_rows, first_band(conv_first), second_band(conv_second),
                                 jnp.asarray(edge_mask(), jnp.bfloat16), emb, patch_weight)
 
-    row_count = token_rows.shape[0]
-    projected = jnp.dot(normed, lax.all_gather(attend_weight, "tile", axis=1, tiled=True),
-                        preferred_element_type=jnp.float32).astype(jnp.bfloat16)
-    cube_count = row_count // frames
-    projected = projected.reshape(frames, cube_count, 3, HEADS, HD)
-    keys_values = lax.all_gather(projected[:, :, 1:], "tm", axis=0, tiled=True)
-    attended = attend_frames(projected[:, :, 0], keys_values[:, :, 0], keys_values[:, :, 1],
-                             lax.axis_index("tm") * frames)
-    attended_rows = attended.reshape(row_count, D)
+    attended_rows = attend(normed, head_weights(attend_weight))
     mixed_terms = jnp.dot(attended_rows, lax.all_gather(mixing_weight, "tile", axis=1, tiled=True),
                           preferred_element_type=jnp.float32)
     residual = token_rows.astype(jnp.float32) + mixed_terms

time: 203 us -> 120 us (0.59)
  waiting for transfers between devices: 108 us -> 21.4 us
  Pallas kernels: 20.8 us -> 43.6 us
  matrix products: 14.7 us -> 3.38 us
  other arithmetic: 11 us -> 5.13 us
  local copies, waits for them, and re-layouts: 25.9 us -> 20.5 us
  starting transfers between devices: 5.52 us -> 8.65 us
    all_gather x2 -> x1, waiting for transfers between devices: 70.8 us -> 17.7 us  [head_weights(): quarter = lax.all_gather(quarter, 'tile', axis=1, tiled=True)]
    all_gather x1, waiting for transfers between devices: 36.2 us -> 3.73 us  [local(): lax.all_gather(mixing_weight, 'tile', axis=1, tiled=True)]
    pallas_call x0 -> x1, Pallas kernels: none -> 22.7 us  [attend(): pl.pallas_call(attend_kernel, in_specs=[vmem] * 5, out_specs=vmem, out_sh...]
    dot_general x3 -> x0, matrix products: 10.6 us -> none  [the longest x1 6.2 us: attend_frames(): jnp.einsum('tnhd,smhd->htnsm', query, keys_all, preferred_element_type=jn...]
    reshape x1 -> x0, local copies, waits for them, and re-layouts: 5.26 us -> none  [attend_frames(): scores = scores.reshape(scores.shape[0], query.shape[0], query.shape[1], -1)]
    reduce_sum x1 -> x0, other arithmetic: 4.49 us -> none  [attend_frames(): jnp.sum(shifted, axis=-1, keepdims=True)]
    dynamic_slice x0 -> x2, local copies, waits for them, and re-layouts: none -> 3.27 us  [the longest x1 1.7 us: head_weights(): quarter = lax.dynamic_slice_in_dim(attend_weight, me * 256, 256, axis=0)]
    ppermute x0 -> x3, starting transfers between devices: none -> 2.44 us  [head_weights(): lax.ppermute(columns(other), 'tm', [(m, m ^ i + 1) for m in range(4)])]
  transfers between devices with their start and end apart: 5 -> 7, of which waited for: 3 -> 2; matrix products, arithmetic and copies ran while one was open for 22% -> 20% of each run, Pallas kernels for 10% -> 37%
where the time goes in v2:
time: 120 us; the launch traced here: 118 us
  Pallas kernels  43.6 us (36%)
  waiting for transfers between devices  21.4 us (18%)
  local copies, waits for them, and re-layouts  20.5 us (17%)
  between operations  14.8 us (12%)
  starting transfers between devices  8.65 us (7%)
  other arithmetic  5.13 us (4%)
  matrix products  3.38 us (3%)
    pallas_call x1, Pallas kernels, attend(): pl.pallas_call(attend_kernel, in_specs=[vmem] * 5, out_specs=vmem, out_sh...  22.7 us
    pallas_call x1, Pallas kernels, encode(): pl.pallas_call(encode_kernel, grid=(planes - 2,), in_specs=[pl.BlockSpec(...  20.8 us
    all_gather x1, waiting for transfers between devices, head_weights(): quarter = lax.all_gather(quarter, 'tile', axis=1, tiled=True)  17.7 us
    broadcast_in_dim x10, local copies, waits for them, and re-layouts, banded(): total = total + jnp.where(code == float(j * TAPS + k), taps(j, k), 0.0)  4.69 us
    reshape x1, local copies, waits for them, and re-layouts, local(): rows = volume.reshape(frames, width, depth // 8, 8, height // 8, 8)  4.32 us
    ppermute x1, starting transfers between devices, local(): lax.ppermute(rows[-2:], 'tile', [(i, i + 1) for i in range(tiles - 1)])  4.25 us
    all_gather x1, waiting for transfers between devices, local(): lax.all_gather(mixing_weight, 'tile', axis=1, tiled=True)  3.73 us
    transpose x1, local copies, waits for them, and re-layouts, local(): rows = rows.transpose(1, 3, 5, 0, 2, 4).reshape(width, 64, 128)  2.86 us
  transfers between devices with their start and end apart: 7, of which 2 were waited for; matrix products, arithmetic and copies ran while one was open for 20% of the time, Pallas kernels for 37%

profile of v2, /device:TPU:3, one launch (start us, length us, event | category | flops | bytes accessed | tf_op | source)
XLA Modules:
  0.0 117.5 jit_solution(7625033434525713629)
XLA Ops:
  6.5 1.7 %constant_dynamic-slice_fusion.12 = bf16[256,384]{1,0:T(8,128)(2,1)} fusion(bf16[1024,384]{1,0:T(8,128)(2,1)} %param.19, s32[]{:T(128)S(6)} %select_n.181), kind=kLoop, calls=%fused_computation.78 | loop fusion | bytes 393220 | tf_op jit(solution)/shard_map/dynamic_slice | solution.py:301
  8.3 4.3 %reshape.327 = bf16[4,8,2,8,16,8]{5,4,3,2,1,0:T(8,128)(2,1)} reshape(bf16[4,8,16,128]{3,2,1,0:T(8,128)(2,1)} %param.13) | data formatting | bytes 262144 | tf_op jit(solution)/shard_map/reshape | solution.py:321
  12.6 1.4 %fusion.19 = (bf16[2,8,8,4,2,16]{2,5,1,4,0,3:T(8,128)(2,1)S(1)}, bf16[2,8,8,4,2,16]{2,5,1,4,0,3:T(8,128)(2,1)S(1)}) fusion(bf16[8,8,8,4,2,16]{2,5,1,4,0,3:T(8,128)(2,1)} %bitcast.133), kind=kLoop, calls=%fused_computation.84 | loop fusion | bytes 131072 | tf_op jit(solution)/shard_map/slice | solution.py:323
  14.4 0.8 slice.78
  15.2 1.9 %collective-permute-start.1 = (bf16[2,64,128]{2,1,0:T(8,128)(2,1)}, bf16[2,64,128]{2,1,0:T(8,128)(2,1)S(1)}, u32[]{:S(2)}, u32[]{:S(2)}) collective-permute-start(bf16[2,64,128]{2,1,0:T(8,128)(2,1)} %slice.78), channel_id=1, source_target_pairs={{4,0},{8,4},{12,8},{16,12},{20,16},{24,20},{28,24},{5,1},{9,5},{13... | collective-permute-start | bytes 98312 | tf_op jit(solution)/shard_map/ppermute | solution.py:324
  17.4 0.8 slice.76
  18.1 4.2 %collective-permute-start = (bf16[2,64,128]{2,1,0:T(8,128)(2,1)}, bf16[2,64,128]{2,1,0:T(8,128)(2,1)}, u32[]{:S(2)}, u32[]{:S(2)}) collective-permute-start(bf16[2,64,128]{2,1,0:T(8,128)(2,1)} %slice.76), channel_id=1, source_target_pairs={{0,4},{4,8},{8,12},{12,16},{16,20},{20,24},{24,28},{1,5},{5,9},{9,... | collective-permute-start | bytes 98312 | tf_op jit(solution)/shard_map/ppermute | solution.py:323
  23.0 0.6 fusion.21
  24.4 0.6 add_convert_fusion.2
  25.7 0.6 add_convert_fusion.1
  26.4 0.3 add_sine_fusion
  26.9 0.4 add_convert_fusion
  27.4 2.9 %copy.18 = bf16[8,8,8,4,2,16]{5,4,3,2,1,0:T(2,128)(2,1)S(1)} copy(bf16[8,8,8,4,2,16]{2,5,1,4,0,3:T(8,128)(2,1)} %bitcast.134) | data formatting | bytes 262144 | tf_op jit(solution)/shard_map/transpose | solution.py:322
  30.4 0.7 reshape.328
  31.2 0.8 broadcast_in_dim.374
  31.9 0.8 broadcast_in_dim.368
  32.7 0.8 broadcast_in_dim.362
  33.5 0.8 broadcast_in_dim.356
  34.2 0.8 broadcast_in_dim.350
  35.0 0.8 broadcast_in_dim.344
  35.9 1.6 %fusion.1.t2_ref = bf16[3,640,256]{2,1,0:T(8,128)(2,1)S(1)} fusion(f32[3,16,256]{2,1,0:T(8,128)S(1)} %get-tuple-element.24, f32[3,16,256]{2,1,0:T(8,128)S(1)} %get-tuple-element.25, f32[3,16,256]{2,1,0:T(8,128)S(1)} %get-tuple-element.26, f32[3,16,256]{2,1,0:T(8,128)S(1)} %get-tuple-element.27, f32[3,16,256]{2,1,0:T(8,128)S(1)} %get-tuple-element.28, ...), kind=kLoop, calls=%fused_computation.2 | loop fusion | flops 8847360 | bytes 2899968 | tf_op jit(solution)/shard_map/convert_element_type | solution.py:71
  37.6 0.8 pad_maximum_fusion.4.vol_ref
  38.4 17.7 %all-gather.3.cloned.1.call-done = bf16[256,3072]{1,0:T(8,128)(2,1)} async-done(((bf16[256,384]{1,0:T(8,128)(2,1)}), bf16[256,3072]{1,0:T(8,128)(2,1)}) %all-gather.3.cloned.1.call-update) | async-done | bytes 1572880 | tf_op jit(solution)/shard_map/all_gather | solution.py:302
  56.0 1.6 %constant_dynamic-slice_fusion.2 = (bf16[256,256]{1,0:T(8,128)(2,1)S(1)}, bf16[256,256]{1,0:T(8,128)(2,1)S(1)}, bf16[256,256]{1,0:T(8,128)(2,1)S(1)}, bf16[256,2...) fusion(bf16[256,3072]{1,0:T(8,128)(2,1)} %all-gather.3.cloned.1, ...), kind=kLoop, calls=%fused_computation.68 | loop fusion | bytes 3145776 | tf_op jit(solution)/shard_map/dynamic_slice | solution.py:306
  57.6 0.7 collective-permute-start.2
  58.3 1.3 %collective-permute-start.3 = (bf16[256,768]{1,0:T(8,128)(2,1)S(1)}, bf16[256,768]{1,0:T(8,128)(2,1)S(1)}, u32[]{:S(2)}, u32[]{:S(2)}) collective-permute-start(bf16[256,768]{1,0:T(8,128)(2,1)S(1)} %pad_maximum_fusion.2), channel_id=1, source_target_pairs={{0,2},{1,3},{2,0},{3,1},{4,6},{5,7},{6,4},{7,5},{8,10},{9,11},{10,... | collective-permute-start | bytes 1179656 | tf_op jit(solution)/shard_map/ppermute | solution.py:312
  59.6 0.5 collective-permute-start.4
  60.1 20.8 %encode.1 = (bf16[128,1024]{1,0:T(8,128)(2,1)S(1)}, bf16[128,1024]{1,0:T(8,128)(2,1)S(1)}) custom-call(s32[2]{0:T(128)S(1)} %pad_add_fusion.place_ref, bf16[12,64,128]{2,1,0:T(8,128)(2,1)S(1)} %pad_maximum_fusion.4.vol_ref, bf16[256,640]{1,0:T(8,128)(2,1)S(1)} %pad.5.t1_ref, bf16[3,640,256]{2,1,0:T(8,128)(2,1)S(1)} %fusion.1.t2_ref, ...), custom_call_target="tpu_custom_call" | custom-call | flops 8000000000 | bytes 20971520 | tf_op jit(solution)/shard_map/encode/pallas_call | solution.py:162
  81.1 22.7 %attend.1 = bf16[128,1024]{1,0:T(8,128)(2,1)S(1)} custom-call(bf16[128,1024]{1,0:T(8,128)(2,1)S(1)} %get-tuple-element.8.norm_ref, bf16[256,768]{1,0:T(8,128)(2,1)S(1)} %pad_maximum_fusion.w0_ref, bf16[256,768]{1,0:T(8,128)(2,1)S(1)} %collective-permute-done.2.w1_ref, bf16[256,768]{1,0:T(8,128)(2,1)S(1)} %collective-permute-done.3.w2_ref, ...), custom_call_target="tpu_custom_call" | custom-call | flops 1000000000 | bytes 2097152 | tf_op jit(solution)/shard_map/attend/pallas_call | solution.py:280
  103.8 3.7 %all-gather.5.cloned.1.call-done = bf16[1024,1024]{1,0:T(8,128)(2,1)} async-done(((bf16[1024,128]{1,0:T(8,128)(2,1)}), bf16[1024,1024]{1,0:T(8,128)(2,1)}) %all-gather.5.cloned.1.call-update) | async-done | bytes 2097168 | tf_op jit(solution)/shard_map/all_gather | solution.py:336
  107.5 2.1 %multiply_reduce_fusion = (f32[128]{0:T(128)S(1)}, f32[128,1024]{1,0:T(8,128)S(1)}) fusion(bf16[128,1024]{1,0:T(8,128)(2,1)S(1)} %get-tuple-element.7, bf16[128,1024]{1,0:T(8,128)(2,1)S(1)} %attend.1, bf16[1024,1024]{1,0:T(8,128)(2,1)} %all-gather.5.cloned.1.call-done), kind=kOutput, calls=%fused_computation.22 | convolution fusion | flops 268959616 | bytes 3146240 | tf_op jit(solution)/shard_map/dot_general | solution.py:336
  109.7 1.0 convolution_convert_fusion
  (78 shorter events, 2.2 us)
Async XLA Ops:
  6.5 103.1 %copy-start = (bf16[1024,512]{1,0:T(8,128)(2,1)S(1)}, bf16[1024,512]{1,0:T(8,128)(2,1)}, u32[]{:S(2)}) copy-start(bf16[1024,512]{1,0:T(8,128)(2,1)} %param.21) | copy-start | bytes 3145732
  6.5 49.5 %all-gather.3.cloned.1.call-start = ((), (), s32[]{:S(2)}) async-start(), calls=%async_computation | async-start | bytes 1769472 | tf_op jit(solution)/shard_map/all_gather | solution.py:302
  8.3 99.3 %all-gather.5.cloned.1.call-start = ((), (), s32[]{:S(2)}) async-start(), calls=%async_computation.1 | async-start | bytes 2359296 | tf_op jit(solution)/shard_map/all_gather | solution.py:336
  12.6 9.8 %copy-start.15 = (bf16[16,1,3,3,3]{0,4,3,2,1:T(4,128)(2,1)S(1)}, bf16[16,1,3,3,3]{0,4,3,2,1:T(4,128)(2,1)}, u32[]{:S(2)}) copy-start(bf16[16,1,3,3,3]{0,4,3,2,1:T(4,128)(2,1)} %param.16) | copy-start | bytes 2596
  14.1 8.9 %copy-start.17 = (s32[3]{0:T(128)S(1)}, s32[3]{0:T(128)}, u32[]{:S(2)}) copy-start(s32[3]{0:T(128)} %param.15) | copy-start | bytes 40
  14.1 10.9 %copy-start.18 = (s32[4]{0:T(128)S(1)}, s32[4]{0:T(128)}, u32[]{:S(2)}) copy-start(s32[4]{0:T(128)} %param.14) | copy-start | bytes 52
  14.1 10.9 %copy-start.2 = (bf16[16,16,3,3,3]{1,0,4,3,2:T(8,128)(2,1)S(1)}, bf16[16,16,3,3,3]{1,0,4,3,2:T(8,128)(2,1)}, u32[]{:S(2)}) copy-start(bf16[16,16,3,3,3]{1,0,4,3,2:T(8,128)(2,1)} %param.17) | copy-start | bytes 41476
  14.1 10.9 %copy-start.16 = (bf16[16,256,1,1,1]{1,0,4,3,2:T(8,128)(2,1)S(1)}, bf16[16,256,1,1,1]{1,0,4,3,2:T(8,128)(2,1)}, u32[]{:S(2)}) copy-start(bf16[16,256,1,1,1]{1,0,4,3,2:T(8,128)(2,1)} %constant.161) | copy-start | bytes 24580
  15.2 22.4 %collective-permute-start.1 = (bf16[2,64,128]{2,1,0:T(8,128)(2,1)}, bf16[2,64,128]{2,1,0:T(8,128)(2,1)S(1)}, u32[]{:S(2)}, u32[]{:S(2)}) collective-permute-start(bf16[2,64,128]{2,1,0:T(8,128)(2,1)} %slice.78), channel_id=1, source_target_pairs={{4,0},{8,4},{12,8},{16,12},{20,16},{24,20},{28,24},{5,1},{9,5},{13... | collective-permute-start | bytes 98312 | tf_op jit(solution)/shard_map/ppermute | solution.py:324
  18.1 19.4 %collective-permute-start = (bf16[2,64,128]{2,1,0:T(8,128)(2,1)}, bf16[2,64,128]{2,1,0:T(8,128)(2,1)}, u32[]{:S(2)}, u32[]{:S(2)}) collective-permute-start(bf16[2,64,128]{2,1,0:T(8,128)(2,1)} %slice.76), channel_id=1, source_target_pairs={{0,4},{4,8},{8,12},{12,16},{16,20},{20,24},{24,28},{1,5},{5,9},{9,... | collective-permute-start | bytes 98312 | tf_op jit(solution)/shard_map/ppermute | solution.py:323
  22.5 4.3 %copy-start.3 = (pred[72,640]{1,0:T(8,128)(4,1)S(1)}, pred[72,640]{1,0:T(8,128)(4,1)}, u32[]{:S(2)}) copy-start(pred[72,640]{1,0:T(8,128)(4,1)} %constant.142) | copy-start | bytes 138244
  22.5 4.3 %copy-start.4 = (pred[72,640]{1,0:T(8,128)(4,1)S(1)}, pred[72,640]{1,0:T(8,128)(4,1)}, u32[]{:S(2)}) copy-start(pred[72,640]{1,0:T(8,128)(4,1)} %constant.141) | copy-start | bytes 138244
  22.5 4.3 %copy-start.5 = (pred[72,640]{1,0:T(8,128)(4,1)S(1)}, pred[72,640]{1,0:T(8,128)(4,1)}, u32[]{:S(2)}) copy-start(pred[72,640]{1,0:T(8,128)(4,1)} %constant.140) | copy-start | bytes 138244
  22.5 4.3 %copy-start.6 = (pred[72,640]{1,0:T(8,128)(4,1)S(1)}, pred[72,640]{1,0:T(8,128)(4,1)}, u32[]{:S(2)}) copy-start(pred[72,640]{1,0:T(8,128)(4,1)} %constant.139) | copy-start | bytes 138244
  22.5 4.3 %copy-start.7 = (pred[72,640]{1,0:T(8,128)(4,1)S(1)}, pred[72,640]{1,0:T(8,128)(4,1)}, u32[]{:S(2)}) copy-start(pred[72,640]{1,0:T(8,128)(4,1)} %constant.138) | copy-start | bytes 138244
  22.5 4.3 %copy-start.8 = (pred[72,640]{1,0:T(8,128)(4,1)S(1)}, pred[72,640]{1,0:T(8,128)(4,1)}, u32[]{:S(2)}) copy-start(pred[72,640]{1,0:T(8,128)(4,1)} %constant.137) | copy-start | bytes 138244
  22.6 4.3 %copy-start.9 = (pred[72,640]{1,0:T(8,128)(4,1)S(1)}, pred[72,640]{1,0:T(8,128)(4,1)}, u32[]{:S(2)}) copy-start(pred[72,640]{1,0:T(8,128)(4,1)} %constant.136) | copy-start | bytes 138244
  22.6 4.3 %copy-start.10 = (pred[72,640]{1,0:T(8,128)(4,1)S(1)}, pred[72,640]{1,0:T(8,128)(4,1)}, u32[]{:S(2)}) copy-start(pred[72,640]{1,0:T(8,128)(4,1)} %constant.135) | copy-start | bytes 138244
  22.6 4.3 %copy-start.11 = (pred[72,640]{1,0:T(8,128)(4,1)S(1)}, pred[72,640]{1,0:T(8,128)(4,1)}, u32[]{:S(2)}) copy-start(pred[72,640]{1,0:T(8,128)(4,1)} %constant.134) | copy-start | bytes 138244
  30.3 5.4 %copy-start.14 = (pred[40,256]{1,0:T(8,128)(4,1)S(1)}, pred[40,256]{1,0:T(8,128)(4,1)}, u32[]{:S(2)}) copy-start(pred[40,256]{1,0:T(8,128)(4,1)} %constant.148) | copy-start | bytes 30724
  30.3 5.5 %copy-start.13 = (pred[40,256]{1,0:T(8,128)(4,1)S(1)}, pred[40,256]{1,0:T(8,128)(4,1)}, u32[]{:S(2)}) copy-start(pred[40,256]{1,0:T(8,128)(4,1)} %constant.146) | copy-start | bytes 30724
  30.3 5.5 %copy-start.12 = (pred[40,256]{1,0:T(8,128)(4,1)S(1)}, pred[40,256]{1,0:T(8,128)(4,1)}, u32[]{:S(2)}) copy-start(pred[40,256]{1,0:T(8,128)(4,1)} %constant.144) | copy-start | bytes 30724
  57.6 2.6 %copy-start.1 = (bf16[512,128]{1,0:T(8,128)(2,1)S(1)}, bf16[512,128]{1,0:T(8,128)(2,1)}, u32[]{:S(2)}) copy-start(bf16[512,128]{1,0:T(8,128)(2,1)} %constant.131.clone.mask_ref) | copy-start | bytes 393220
  57.6 23.4 %collective-permute-start.2 = (bf16[256,768]{1,0:T(8,128)(2,1)S(1)}, bf16[256,768]{1,0:T(8,128)(2,1)S(1)}, u32[]{:S(2)}, u32[]{:S(2)}) collective-permute-start(bf16[256,768]{1,0:T(8,128)(2,1)S(1)} %pad_maximum_fusion.1), channel_id=1, source_target_pairs={{0,1},{1,0},{2,3},{3,2},{4,5},{5,4},{6,7},{7,6},{8,9},{9,8},{10,11... | collective-permute-start | bytes 1179656 | tf_op jit(solution)/shard_map/ppermute | solution.py:312
  58.3 22.7 %collective-permute-start.3 = (bf16[256,768]{1,0:T(8,128)(2,1)S(1)}, bf16[256,768]{1,0:T(8,128)(2,1)S(1)}, u32[]{:S(2)}, u32[]{:S(2)}) collective-permute-start(bf16[256,768]{1,0:T(8,128)(2,1)S(1)} %pad_maximum_fusion.2), channel_id=1, source_target_pairs={{0,2},{1,3},{2,0},{3,1},{4,6},{5,7},{6,4},{7,5},{8,10},{9,11},{10,... | collective-permute-start | bytes 1179656 | tf_op jit(solution)/shard_map/ppermute | solution.py:312
  59.6 21.4 %collective-permute-start.4 = (bf16[256,768]{1,0:T(8,128)(2,1)S(1)}, bf16[256,768]{1,0:T(8,128)(2,1)S(1)}, u32[]{:S(2)}, u32[]{:S(2)}) collective-permute-start(bf16[256,768]{1,0:T(8,128)(2,1)S(1)} %pad_maximum_fusion.3), channel_id=1, source_target_pairs={{0,3},{1,2},{2,1},{3,0},{4,7},{5,6},{6,5},{7,4},{8,11},{9,10},{10,... | collective-permute-start | bytes 1179656 | tf_op jit(solution)/shard_map/ppermute | solution.py:312
Sparse Core Ops, SparseCore 0:
  9.4 46.5 all-gather.2
  58.1 49.4 all-gather.4

commit v3 on v2

--- a/solution.py
+++ b/solution.py
@@ -56,19 +56,21 @@
     return jnp.pad(out, ((0, 256 - out.shape[0]), (0, 0))).astype(jnp.bfloat16)
 
 
-def second_band(conv_second):
+def second_taps(conv_second):
+    col = np.arange(256)
+    taps = conv_second.reshape(CH, CH, 27).transpose(2, 1, 0)
+    expand = jnp.asarray((col[None] // 16 == np.arange(CH)[:, None]).astype(np.float32) * 0.5, jnp.bfloat16)
+    spread = jnp.dot(taps.reshape(-1, CH), expand, preferred_element_type=jnp.float32)
+    return spread.reshape(27, CH, 256)
+
+
+def second_code():
     group_z, group_y = map_places()
     col = np.arange(256)
-    col_z, col_y = (col // 8) % 2, col % 8
-    taps = conv_second.reshape(CH, CH, 27).transpose(2, 1, 0).astype(jnp.float32) * 0.5
-    expand = jnp.asarray((col[None] // 16 == np.arange(CH)[:, None]).astype(np.float32), jnp.bfloat16)
-    spread = jnp.dot(taps.reshape(-1, CH).astype(jnp.bfloat16), expand,
-                     preferred_element_type=jnp.float32)
-    spread = spread.reshape(3, 3, 3, 1, CH, 256)
-    shape = (len(group_z), 1, 1)
-    out = banded(group_z.reshape(shape), group_y.reshape(shape), col_z[None, None],
-                 col_y[None, None], lambda j, k: spread[:, j, k])
-    return out.reshape(3, len(group_z) * CH, 256).astype(jnp.bfloat16)
+    dz = group_z[:, None] - (col // 8 % 2)[None]
+    dy = group_y[:, None] - (col % 8)[None]
+    shared = (dz >= 0) & (dz < TAPS) & (dy >= 0) & (dy < TAPS)
+    return np.where(shared, dz * TAPS + dy, -1).astype(np.float32).reshape(-1, 1, 256)
 
 
 def edge_mask():
@@ -83,14 +85,112 @@
     return np.where(bad, 0.0, 1.0).reshape(512, 128)
 
 
-def encode_kernel(place_ref, vol_ref, t1_ref, t2_ref, mask_ref, emb_ref, w_ref,
-                  tok_ref, norm_ref, win_ref, maps_ref, acc_ref):
+def weight_place(unit):
+    return pl.ds(pl.multiple_of((unit // HEADS) * 256 + (unit % 2) * HD, HD), HD)
+
+
+def share_steps(step, last, attend_ref, own_ref, local_sem, send_sem, recv_sem):
+    tile, member = lax.axis_index("tile"), lax.axis_index("tm")
+    row, col = tile // 2, tile % 2
+    beside = row * 2 + 1 - col
+    column = [((row + d) % 4) * 2 + col for d in (1, 2, 3)]
+
+    def wanted(unit):
+        return (unit % HEADS) // 2 == member
+
+    def remote(src, unit, kind, j, target):
+        return pltpu.make_async_remote_copy(
+            src_ref=src, dst_ref=own_ref.at[:, weight_place(unit)], send_sem=send_sem.at[kind, j],
+            recv_sem=recv_sem.at[kind, j], device_id={"tile": target},
+            device_id_type=pl.DeviceIdType.MESH)
+
+    def own_copies(j):
+        unit = tile * 3 + j
+        src = attend_ref.at[:, j * HD:(j + 1) * HD]
+        out = [remote(src, unit, 0, j, beside)]
+        out += [remote(src, unit, d, j, column[d - 1]) for d in (1, 2, 3)]
+        return out, pltpu.make_async_copy(src, own_ref.at[:, weight_place(unit)], local_sem.at[j])
+
+    def passed_on(d, j):
+        unit = (((row - d) % 4) * 2 + col) * 3 + j
+        return unit, remote(own_ref.at[:, weight_place(unit)], unit, 3 + d, j, beside)
+
+    @pl.when(step == 0)
+    def _():
+        barrier = pltpu.get_barrier_semaphore()
+        for target in [beside] + column:
+            pl.semaphore_signal(barrier, inc=1, device_id={"tile": target},
+                                device_id_type=pl.DeviceIdType.MESH)
+        pl.semaphore_wait(barrier, 4)
+        for j in range(3):
+            @pl.when(wanted(tile * 3 + j))
+            def _():
+                copies, here = own_copies(j)
+                for copy in copies:
+                    copy.start()
+                here.start()
+
+    for d, when in ((1, 4), (3, 5), (2, 6)):
+        @pl.when(step == when)
+        def _():
+            for j in range(3):
+                unit, onward = passed_on(d, j)
+
+                @pl.when(wanted(unit))
+                def _():
+                    remote(attend_ref.at[:, j * HD:(j + 1) * HD], unit, d, j, beside).wait_recv()
+                    onward.start()
+
+    @pl.when(step == last)
+    def _():
+        for j in range(3):
+            @pl.when(wanted(tile * 3 + j))
+            def _():
+                copies, here = own_copies(j)
+                for copy in copies:
+                    copy.wait_send()
+                here.wait()
+
+            for d in (1, 2, 3):
+                unit, onward = passed_on(d, j)
+
+                @pl.when(wanted(unit))
+                def _():
+                    onward.wait_send()
+
+            for kind, back in ((0, 0), (4, 1), (5, 2), (6, 3)):
+                unit = (((row - back) % 4) * 2 + 1 - col) * 3 + j
+
+                @pl.when(wanted(unit))
+                def _():
+                    remote(attend_ref.at[:, j * HD:(j + 1) * HD], unit, kind, j, beside).wait_recv()
+
+
+def encode_kernel(share, *refs):
+    vol_ref, t1_ref, taps_ref, code_ref, mask_ref, emb_ref, w_ref = refs[:7]
+    if share:
+        attend_ref, tok_ref, norm_ref, own_ref = refs[7:11]
+        win_ref, maps_ref, acc_ref, t2_ref = refs[11:15]
+    else:
+        tok_ref, norm_ref, win_ref, maps_ref, acc_ref, t2_ref = refs[7:]
     step = pl.program_id(0)
     last = pl.num_programs(0) - 1
+    if share:
+        share_steps(step, last, attend_ref, own_ref, *refs[15:])
 
     @pl.when(step == 0)
     def _():
         acc_ref[...] = jnp.zeros_like(acc_ref)
+
+        @pl.loop(0, code_ref.shape[0])
+        def _(group):
+            code = code_ref[group]
+            for dx in range(3):
+                total = jnp.zeros((CH, 256), jnp.float32)
+                for tap in range(9):
+                    total += jnp.where(code == float(tap), taps_ref[9 * dx + tap], 0.0)
+                t2_ref[dx, pl.ds(pl.multiple_of(group * CH, CH), CH)] = total.astype(jnp.bfloat16)
+
         row = lax.broadcasted_iota(jnp.int32, (96, 128), 0) % 8
         lane = lax.broadcasted_iota(jnp.int32, (96, 128), 1)
         up_ok = (row >= 6) & (lane % 16 >= 1)
@@ -128,7 +228,8 @@
         maps_ref[slot, 32 * t:32 * t + 16, 0:128] = none
         maps_ref[slot, 400 + 32 * t:416 + 32 * t, 384:512] = none
 
-    outside = ((step == 0) & (place_ref[0] == 0)) | ((step == last) & (place_ref[0] == place_ref[1] - 1))
+    tile = lax.axis_index("tile")
+    outside = ((step == 0) & (tile == 0)) | ((step == last) & (tile == lax.axis_size("tile") - 1))
 
     @pl.when(outside)
     def _():
@@ -155,31 +256,45 @@
         norm_ref[...] = (wide * scale).astype(jnp.bfloat16)
 
 
-def encode(place, volume_rows, t1, t2, mask, emb, patch_weight):
+def encode(volume_rows, t1, taps, emb, patch_weight, attend_weight):
     planes = volume_rows.shape[0]
+    share = attend_weight is not None
     whole = lambda shape: pl.BlockSpec(shape, lambda s: (0,) * len(shape))
     weight = patch_weight.reshape(CH, 8, 4, 16, D)
+    code, mask = jnp.asarray(second_code()), jnp.asarray(edge_mask(), jnp.bfloat16)
+    held = [volume_rows, t1, taps, code, mask, emb]
+    in_specs = [whole(array.shape) for array in held]
+    in_specs.append(pl.BlockSpec((CH, 1, 4, 16, D), lambda s: (0, jnp.maximum(s - 2, 0), 0, 0, 0)))
+    out_specs = [whole((128, D)), whole((128, D))]
+    out_shape = [jax.ShapeDtypeStruct((128, D), jnp.bfloat16)] * 2
+    scratch = [
+        pltpu.VMEM((planes, 144, 128), jnp.float32),
+        pltpu.VMEM((3, 512, 640), jnp.bfloat16),
+        pltpu.VMEM((128, D), jnp.float32),
+        pltpu.VMEM((3, 640, 256), jnp.bfloat16),
+    ]
+    operands = held + [weight]
+    extra = {}
+    if share:
+        operands.append(attend_weight)
+        in_specs.append(pl.BlockSpec(memory_space=pl.ANY))
+        out_specs.append(pl.BlockSpec(memory_space=pl.ANY))
+        out_shape.append(jax.ShapeDtypeStruct((D, 768), jnp.bfloat16))
+        scratch += [pltpu.SemaphoreType.DMA((3,)), pltpu.SemaphoreType.DMA((7, 3)),
+                    pltpu.SemaphoreType.DMA((7, 3))]
+        extra = dict(collective_id=1, has_side_effects=True)
     return pl.pallas_call(
-        encode_kernel,
+        functools.partial(encode_kernel, share),
         grid=(planes - 2,),
-        in_specs=[
-            pl.BlockSpec(memory_space=pltpu.SMEM),
-            whole(volume_rows.shape), whole(t1.shape), whole(t2.shape), whole(mask.shape),
-            whole(emb.shape),
-            pl.BlockSpec((CH, 1, 4, 16, D), lambda s: (0, jnp.maximum(s - 2, 0), 0, 0, 0)),
-        ],
-        out_specs=[whole((128, D)), whole((128, D))],
-        out_shape=[jax.ShapeDtypeStruct((128, D), jnp.bfloat16)] * 2,
-        scratch_shapes=[
-            pltpu.VMEM((planes, 144, 128), jnp.float32),
-            pltpu.VMEM((3, 512, 640), jnp.bfloat16),
-            pltpu.VMEM((128, D), jnp.float32),
-        ],
-        compiler_params=pltpu.CompilerParams(vmem_limit_bytes=40 * 2**20),
+        in_specs=in_specs,
+        out_specs=out_specs,
+        out_shape=out_shape,
+        scratch_shapes=scratch,
+        compiler_params=pltpu.CompilerParams(vmem_limit_bytes=40 * 2**20, **extra),
         cost_estimate=pl.CostEstimate(flops=8 * 10**9, bytes_accessed=20 * 2**20,
                                       transcendentals=5 * 10**6),
         name="encode",
-    )(place, volume_rows, t1, t2, mask, emb, weight)
+    )(*operands)
 
 
 def settle(values_in):
@@ -209,7 +324,7 @@
     return me, (sibling, (me + 2) % 4, (sibling + 2) % 4)
 
 
-def attend_kernel(norm_ref, w0_ref, w1_ref, w2_ref, w3_ref, out_ref, rows_ref, qkv_ref, att_ref,
+def attend_kernel(norm_ref, w_ref, out_ref, rows_ref, qkv_ref, att_ref,
                   back_ref, send_sem, recv_sem, send_back, recv_back):
     me, others = partners()
     barrier = pltpu.get_barrier_semaphore()
@@ -228,10 +343,7 @@
         send.start()
 
     def project(block, source):
-        total = jnp.zeros((128, 768), jnp.float32)
-        for owner, w_ref in zip((me,) + others, (w0_ref, w1_ref, w2_ref, w3_ref)):
-            part = source[:, pl.ds(pl.multiple_of(owner * 256, 256), 256)]
-            total += jnp.dot(part, w_ref[...], preferred_element_type=jnp.float32)
+        total = jnp.dot(source[...], w_ref[...], preferred_element_type=jnp.float32)
         qkv_ref[block] = total.astype(jnp.bfloat16)
 
     project(me, norm_ref)
@@ -279,7 +391,7 @@
     vmem = pl.BlockSpec(memory_space=pltpu.VMEM)
     return pl.pallas_call(
         attend_kernel,
-        in_specs=[vmem] * 5,
+        in_specs=[vmem] * 2,
         out_specs=vmem,
         out_shape=jax.ShapeDtypeStruct((128, D), jnp.bfloat16),
         scratch_shapes=[
@@ -293,7 +405,7 @@
         cost_estimate=pl.CostEstimate(flops=10**9, bytes_accessed=2 * 2**20,
                                       transcendentals=4 * 10**5),
         name="attend",
-    )(normed, *weights)
+    )(normed, weights)
 
 
 def head_weights(attend_weight):
@@ -307,10 +419,12 @@
             axis=1)
 
     me, others = partners()
-    pieces = [columns(me)]
+    weights = jnp.zeros((D, 768), attend_weight.dtype)
+    weights = lax.dynamic_update_slice_in_dim(weights, columns(me), me * 256, axis=0)
     for i, other in enumerate(others):
-        pieces.append(lax.ppermute(columns(other), "tm", [(m, m ^ (i + 1)) for m in range(4)]))
-    return pieces
+        piece = lax.ppermute(columns(other), "tm", [(m, m ^ (i + 1)) for m in range(4)])
+        weights = lax.dynamic_update_slice_in_dim(weights, piece, other * 256, axis=0)
+    return weights
 
 
 def local(volume, frame_index, tile_offset, conv_first, conv_second, patch_weight,
@@ -328,11 +442,13 @@
     space_emb = embed_space(tile_offset, tile_place + jnp.arange(1), jnp.arange(depth // EDGE),
                             jnp.arange(height // EDGE), frequency)
     emb = (time_emb[:, None, :] + space_emb[None]).reshape(-1, D)
-    place = jnp.stack([tile_place, jnp.int32(tiles)]).astype(jnp.int32)
-    token_rows, normed = encode(place, volume_rows, first_band(conv_first), second_band(conv_second),
-                                jnp.asarray(edge_mask(), jnp.bfloat16), emb, patch_weight)
-
-    attended_rows = attend(normed, head_weights(attend_weight))
+    t1, taps = first_band(conv_first), second_taps(conv_second)
+    if tiles == 8 and attend_weight.shape[1] == 3 * HD:
+        token_rows, normed, weights = encode(volume_rows, t1, taps, emb, patch_weight, attend_weight)
+    else:
+        token_rows, normed = encode(volume_rows, t1, taps, emb, patch_weight, None)
+        weights = head_weights(attend_weight)
+    attended_rows = attend(normed, weights)
     mixed_terms = jnp.dot(attended_rows, lax.all_gather(mixing_weight, "tile", axis=1, tiled=True),
                           preferred_element_type=jnp.float32)
     residual = token_rows.astype(jnp.float32) + mixed_terms

time: 120 us -> 124 us (1.033)
  the two profiles are of different devices: /device:TPU:3 before, /device:TPU:19 now
where the time goes in v3:
time: 124 us; the launch traced here: 123 us
  Pallas kernels  75.9 us (61%)
  local copies, waits for them, and re-layouts  18.1 us (15%)
  between operations  14.3 us (12%)
  starting transfers between devices  6.16 us (5%)
  other arithmetic  4.39 us (4%)
  matrix products  4.29 us (3%)
    pallas_call x1, Pallas kernels, encode(): pl.pallas_call(functools.partial(encode_kernel, share), grid=(planes - 2,...  44.9 us
    pallas_call x1, Pallas kernels, attend(): pl.pallas_call(attend_kernel, in_specs=[vmem] * 2, out_specs=vmem, out_sh...  31 us
    transpose x1, local copies, waits for them, and re-layouts, local(): rows = rows.transpose(1, 3, 5, 0, 2, 4).reshape(width, 64, 128)  4.12 us
    ppermute x1, starting transfers between devices, local(): lax.ppermute(rows[-2:], 'tile', [(i, i + 1) for i in range(tiles - 1)])  4.01 us
    reshape x1, local copies, waits for them, and re-layouts, local(): rows = rows.transpose(1, 3, 5, 0, 2, 4).reshape(width, 64, 128)  3.79 us
    reshape x1, local copies, waits for them, and re-layouts, local(): rows = volume.reshape(frames, width, depth // 8, 8, height // 8, 8)  3.53 us
    slice x3, local copies, waits for them, and re-layouts, local(): rows[-2:]  3.38 us
  transfers between devices with their start and end apart: 3, of which 0 were waited for; matrix products, arithmetic and copies ran while one was open for 13% of the time, Pallas kernels for 62%

profile of v3, /device:TPU:19, one launch (start us, length us, event | category | flops | bytes accessed | tf_op | source)
XLA Modules:
  0.0 123.2 jit_solution(15180114014119549509)
XLA Ops:
  6.5 3.5 %reshape.283 = bf16[4,8,2,8,16,8]{5,4,3,2,1,0:T(8,128)(2,1)S(1)} reshape(bf16[4,8,16,128]{3,2,1,0:T(8,128)(2,1)} %param.13) | data formatting | bytes 262144 | tf_op jit(solution)/shard_map/reshape | solution.py:435
  10.1 0.0 copy-start.5
  10.1 1.3 %fusion.6 = (bf16[2,8,8,4,2,16]{2,5,1,4,0,3:T(8,128)(2,1)}, bf16[2,8,8,4,2,16]{2,5,1,4,0,3:T(8,128)(2,1)}) fusion(bf16[8,8,8,4,2,16]{2,5,1,4,0,3:T(8,128)(2,1)S(1)} %bitcast.49), kind=kLoop, calls=%fused_computation.35 | loop fusion | bytes 131072 | tf_op jit(solution)/shard_map/slice | solution.py:437
  11.4 1.3 %copy.20 = bf16[2,8,8,4,2,16]{5,4,3,2,1,0:T(2,128)(2,1)S(1)} copy(bf16[2,8,8,4,2,16]{2,5,1,4,0,3:T(8,128)(2,1)} %get-tuple-element.12) | data formatting | bytes 65536 | tf_op jit(solution)/shard_map/slice | solution.py:438
  12.7 0.8 slice.51
  13.5 2.2 %collective-permute-start.1 = (bf16[2,64,128]{2,1,0:T(8,128)(2,1)}, bf16[2,64,128]{2,1,0:T(8,128)(2,1)S(1)}, u32[]{:S(2)}, u32[]{:S(2)}) collective-permute-start(bf16[2,64,128]{2,1,0:T(8,128)(2,1)} %slice.51), channel_id=1, source_target_pairs={{4,0},{8,4},{12,8},{16,12},{20,16},{24,20},{28,24},{5,1},{9,5},{13... | collective-permute-start | bytes 98312 | tf_op jit(solution)/shard_map/ppermute | solution.py:438
  15.7 1.3 %copy.18 = bf16[2,8,8,4,2,16]{5,4,3,2,1,0:T(2,128)(2,1)S(1)} copy(bf16[2,8,8,4,2,16]{2,5,1,4,0,3:T(8,128)(2,1)} %get-tuple-element.11) | data formatting | bytes 65536 | tf_op jit(solution)/shard_map/slice | solution.py:437
  17.0 0.0 copy-start.6
  17.0 0.8 slice.49
  17.8 4.0 %collective-permute-start = (bf16[2,64,128]{2,1,0:T(8,128)(2,1)}, bf16[2,64,128]{2,1,0:T(8,128)(2,1)}, u32[]{:S(2)}, u32[]{:S(2)}) collective-permute-start(bf16[2,64,128]{2,1,0:T(8,128)(2,1)} %slice.49), channel_id=1, source_target_pairs={{0,4},{4,8},{8,12},{12,16},{16,20},{20,24},{24,28},{1,5},{5,9},{9,... | collective-permute-start | bytes 98312 | tf_op jit(solution)/shard_map/ppermute | solution.py:437
  21.8 0.0 all-gather.2.cloned.1.call-update
  21.9 0.3 tile.9
  22.2 0.1 fusion.7
  22.2 0.7 fusion.8
  23.5 0.7 add_convert_fusion.1
  24.2 0.7 add_convert_fusion.2
  24.9 0.1 multiply_sine_fusion
  24.9 0.2 sine_add_fusion
  25.1 0.2 add_sine_fusion.1
  25.4 0.3 add_sine_fusion
  25.8 1.4 %add_convert_fusion = bf16[3,72,640]{2,1,0:T(8,128)(2,1)S(1)} fusion(f32[3,640]{1,0:T(4,128)S(1)} %get-tuple-element.27, f32[3,640]{1,0:T(4,128)S(1)} %get-tuple-element.28, f32[3,640]{1,0:T(4,128)S(1)} %get-tuple-element.29, f32[3,640]{1,0:T(4,128)S(1)} %get-tuple-element.30, f32[3,640]{1,0:T(4,128)S(1)} %get-tuple-element.31, ...), kind=kLoop, calls=%fused_computation.2 | loop fusion | flops 2488320 | bytes 760320 | tf_op jit(solution)/shard_map/convert
  27.2 1.1 convolution_bitcast_fusion.refs_2_
  28.4 0.0 copy-start.2
  28.4 0.0 copy-start.3
  28.4 4.1 %copy.19 = bf16[8,8,8,4,2,16]{5,4,3,2,1,0:T(2,128)(2,1)} copy(bf16[8,8,8,4,2,16]{2,5,1,4,0,3:T(8,128)(2,1)} %bitcast.50) | data formatting | bytes 262144 | tf_op jit(solution)/shard_map/transpose | solution.py:436
  32.5 3.8 %reshape.284 = bf16[8,64,128]{2,1,0:T(8,128)(2,1)S(1)} reshape(bf16[8,8,8,4,2,16]{5,4,3,2,1,0:T(2,128)(2,1)} %copy.19) | data formatting | bytes 262144 | tf_op jit(solution)/shard_map/reshape | solution.py:436
  36.4 0.8 pad_maximum_fusion.refs_0_
  37.2 44.9 %encode.1 = (bf16[128,1024]{1,0:T(8,128)(2,1)S(1)}, bf16[128,1024]{1,0:T(8,128)(2,1)S(1)}, bf16[1024,768]{1,0:T(8,128)(2,1)S(1)}) custom-call(bf16[12,64,128]{2,1,0:T(8,128)(2,1)S(1)} %pad_maximum_fusion.refs_0_, bf16[256,640]{1,0:T(8,128)(2,1)S(1)} %pad.5.refs_1_, f32[27,16,256]{2,1,0:T(8,128)S(1)} %convolution_bitcast_fusion.refs_2_, ...), custom_call_target="tpu_custom_call" | custom-call | flops 8000000000 | bytes 20971520 | tf_op jit(solution)/shard_map/encode/pallas_call | solution.py:286
  82.1 31.0 %attend.1 = bf16[128,1024]{1,0:T(8,128)(2,1)S(1)} custom-call(bf16[128,1024]{1,0:T(8,128)(2,1)S(1)} %get-tuple-element.9.norm_ref, bf16[1024,768]{1,0:T(8,128)(2,1)S(1)} %get-tuple-element.10.w_ref), custom_call_target="tpu_custom_call" | custom-call | flops 1000000000 | bytes 2097152 | tf_op jit(solution)/shard_map/attend/pallas_call | solution.py:392
  113.2 0.0 all-gather.2.cloned.1.call-done
  113.2 2.1 %multiply_reduce_fusion = (f32[128]{0:T(128)S(1)}, f32[128,1024]{1,0:T(8,128)S(1)}) fusion(bf16[128,1024]{1,0:T(8,128)(2,1)S(1)} %get-tuple-element.8, bf16[128,1024]{1,0:T(8,128)(2,1)S(1)} %attend.1, bf16[1024,1024]{1,0:T(8,128)(2,1)} %all-gather.2.cloned.1.call-done), kind=kOutput, calls=%fused_computation.4 | convolution fusion | flops 268959616 | bytes 3146240 | tf_op jit(solution)/shard_map/dot_general | solution.py:452
  115.3 1.0 convolution_convert_fusion
  (31 shorter events, 0.2 us)
Async XLA Ops:
  6.5 108.8 %copy-start = (bf16[1024,512]{1,0:T(8,128)(2,1)S(1)}, bf16[1024,512]{1,0:T(8,128)(2,1)}, u32[]{:S(2)}) copy-start(bf16[1024,512]{1,0:T(8,128)(2,1)} %param.21) | copy-start | bytes 3145732
  6.5 106.6 %all-gather.2.cloned.1.call-start = ((), (), s32[]{:S(2)}) async-start(), calls=%async_computation | async-start | bytes 2359296 | tf_op jit(solution)/shard_map/all_gather | solution.py:452
  10.1 7.7 %copy-start.4 = (bf16[4,8,2,8,16,8]{5,4,3,2,1,0:T(8,128)(2,1)}, bf16[4,8,2,8,16,8]{5,4,3,2,1,0:T(8,128)(2,1)S(1)}, u32[]{:S(2)}) copy-start(bf16[4,8,2,8,16,8]{5,4,3,2,1,0:T(8,128)(2,1)S(1)} %reshape.283) | copy-start | bytes 393220
  10.1 11.7 %copy-start.5 = (bf16[16,1,3,3,3]{0,4,3,2,1:T(4,128)(2,1)S(1)}, bf16[16,1,3,3,3]{0,4,3,2,1:T(4,128)(2,1)}, u32[]{:S(2)}) copy-start(bf16[16,1,3,3,3]{0,4,3,2,1:T(4,128)(2,1)} %param.16) | copy-start | bytes 2596
  11.4 10.8 %copy-start.7 = (s32[3]{0:T(128)S(1)}, s32[3]{0:T(128)}, u32[]{:S(2)}) copy-start(s32[3]{0:T(128)} %param.15) | copy-start | bytes 40
  11.4 12.8 %copy-start.8 = (s32[4]{0:T(128)S(1)}, s32[4]{0:T(128)}, u32[]{:S(2)}) copy-start(s32[4]{0:T(128)} %param.14) | copy-start | bytes 52
  13.5 22.8 %collective-permute-start.1 = (bf16[2,64,128]{2,1,0:T(8,128)(2,1)}, bf16[2,64,128]{2,1,0:T(8,128)(2,1)S(1)}, u32[]{:S(2)}, u32[]{:S(2)}) collective-permute-start(bf16[2,64,128]{2,1,0:T(8,128)(2,1)} %slice.51), channel_id=1, source_target_pairs={{4,0},{8,4},{12,8},{16,12},{20,16},{24,20},{28,24},{5,1},{9,5},{13... | collective-permute-start | bytes 98312 | tf_op jit(solution)/shard_map/ppermute | solution.py:438
  17.0 10.2 %copy-start.6 = (bf16[16,256,1]{1,0,2:T(8,128)(2,1)S(1)}, bf16[16,256,1]{1,0,2:T(8,128)(2,1)}, u32[]{:S(2)}) copy-start(bf16[16,256,1]{1,0,2:T(8,128)(2,1)} %constant.91) | copy-start | bytes 24580
  17.8 18.6 %collective-permute-start = (bf16[2,64,128]{2,1,0:T(8,128)(2,1)}, bf16[2,64,128]{2,1,0:T(8,128)(2,1)}, u32[]{:S(2)}, u32[]{:S(2)}) collective-permute-start(bf16[2,64,128]{2,1,0:T(8,128)(2,1)} %slice.49), channel_id=1, source_target_pairs={{0,4},{4,8},{8,12},{12,16},{16,20},{20,24},{24,28},{1,5},{5,9},{9,... | collective-permute-start | bytes 98312 | tf_op jit(solution)/shard_map/ppermute | solution.py:437
  28.4 8.8 %copy-start.1 = (bf16[1024,384]{1,0:T(8,128)(2,1)S(1)}, bf16[1024,384]{1,0:T(8,128)(2,1)}, u32[]{:S(2)}) copy-start(bf16[1024,384]{1,0:T(8,128)(2,1)} %refs_7_.1) | copy-start | bytes 2359300
  28.4 8.8 %copy-start.2 = (bf16[512,128]{1,0:T(8,128)(2,1)S(1)}, bf16[512,128]{1,0:T(8,128)(2,1)}, u32[]{:S(2)}) copy-start(bf16[512,128]{1,0:T(8,128)(2,1)} %constant.79.clone.refs_4_) | copy-start | bytes 393220
  28.4 8.8 %copy-start.3 = (f32[40,1,256]{2,1,0:T(1,128)S(1)}, f32[40,1,256]{2,1,0:T(1,128)}, u32[]{:S(2)}) copy-start(f32[40,1,256]{2,1,0:T(1,128)} %constant.78.clone.refs_3_) | copy-start | bytes 122884
Sparse Core Ops, SparseCore 0:
  21.9 65.4 all-gather.1

commit v4 on v3

--- a/solution.py
+++ b/solution.py
@@ -58,9 +58,9 @@
 
 def second_taps(conv_second):
     col = np.arange(256)
-    taps = conv_second.reshape(CH, CH, 27).transpose(2, 1, 0)
+    taps = conv_second.transpose(2, 3, 4, 0, 1).reshape(27, CH, CH)
     expand = jnp.asarray((col[None] // 16 == np.arange(CH)[:, None]).astype(np.float32) * 0.5, jnp.bfloat16)
-    spread = jnp.dot(taps.reshape(-1, CH), expand, preferred_element_type=jnp.float32)
+    spread = lax.dot_general(taps, expand, (((1,), (0,)), ((), ())), preferred_element_type=jnp.float32)
     return spread.reshape(27, CH, 256)
 
 
@@ -85,35 +85,50 @@
     return np.where(bad, 0.0, 1.0).reshape(512, 128)
 
 
-def weight_place(unit):
-    return pl.ds(pl.multiple_of((unit // HEADS) * 256 + (unit % 2) * HD, HD), HD)
-
-
-def share_steps(step, last, attend_ref, own_ref, local_sem, send_sem, recv_sem):
+def share_steps(step, last, vol_ref, attend_ref, mixing_ref, own_ref, mix_ref, halo_ref, halo_send,
+                halo_recv, local_sem, send_sem, recv_sem):
     tile, member = lax.axis_index("tile"), lax.axis_index("tm")
+    ends = lax.axis_size("tile") - 1
     row, col = tile // 2, tile % 2
     beside = row * 2 + 1 - col
     column = [((row + d) % 4) * 2 + col for d in (1, 2, 3)]
-
-    def wanted(unit):
-        return (unit % HEADS) // 2 == member
-
-    def remote(src, unit, kind, j, target):
+    far = tile - 1 + 2 * col
+    has_far = ((col == 0) & (tile > 0)) | ((col == 1) & (tile < ends))
+    mine = pl.ds(pl.multiple_of(member * 256, 256), 256)
+
+    def wanted(owner, j):
+        return ((owner * 3 + j) % HEADS) // 2 == member if j < 3 else member >= 0
+
+    def block(owner, j):
+        if j == 3:
+            return mix_ref.at[owner]
+        unit = owner * 3 + j
+        return own_ref.at[(unit // HEADS) * 2 + unit % 2]
+
+    def source(j):
+        return mixing_ref.at[mine] if j == 3 else attend_ref.at[:, j * HD:(j + 1) * HD]
+
+    def remote(src, owner, kind, j, target):
         return pltpu.make_async_remote_copy(
-            src_ref=src, dst_ref=own_ref.at[:, weight_place(unit)], send_sem=send_sem.at[kind, j],
+            src_ref=src, dst_ref=block(owner, j), send_sem=send_sem.at[kind, j],
             recv_sem=recv_sem.at[kind, j], device_id={"tile": target},
             device_id_type=pl.DeviceIdType.MESH)
 
     def own_copies(j):
-        unit = tile * 3 + j
-        src = attend_ref.at[:, j * HD:(j + 1) * HD]
-        out = [remote(src, unit, 0, j, beside)]
-        out += [remote(src, unit, d, j, column[d - 1]) for d in (1, 2, 3)]
-        return out, pltpu.make_async_copy(src, own_ref.at[:, weight_place(unit)], local_sem.at[j])
+        out = [remote(source(j), tile, d, j, column[d - 1]) for d in (1, 2, 3)]
+        out.append(remote(source(j), tile, 0, j, beside))
+        return out, pltpu.make_async_copy(source(j), block(tile, j), local_sem.at[j])
 
     def passed_on(d, j):
-        unit = (((row - d) % 4) * 2 + col) * 3 + j
-        return unit, remote(own_ref.at[:, weight_place(unit)], unit, 3 + d, j, beside)
+        owner = ((row - d) % 4) * 2 + col
+        return owner, remote(block(owner, j), owner, 3 + d, j, beside)
+
+    def halo(side, target):
+        src = vol_ref.at[vol_ref.shape[0] - 2:] if side == 0 else vol_ref.at[:2]
+        return pltpu.make_async_remote_copy(
+            src_ref=src, dst_ref=halo_ref.at[side], send_sem=halo_send.at[side],
+            recv_sem=halo_recv.at[side], device_id={"tile": target},
+            device_id_type=pl.DeviceIdType.MESH)
 
     @pl.when(step == 0)
     def _():
@@ -121,30 +136,72 @@
         for target in [beside] + column:
             pl.semaphore_signal(barrier, inc=1, device_id={"tile": target},
                                 device_id_type=pl.DeviceIdType.MESH)
-        pl.semaphore_wait(barrier, 4)
-        for j in range(3):
-            @pl.when(wanted(tile * 3 + j))
+
+        @pl.when(has_far)
+        def _():
+            pl.semaphore_signal(barrier, inc=1, device_id={"tile": far},
+                                device_id_type=pl.DeviceIdType.MESH)
+            pl.semaphore_wait(barrier, 5)
+
+        @pl.when(jnp.logical_not(has_far))
+        def _():
+            pl.semaphore_wait(barrier, 4)
+
+        @pl.when(tile < ends)
+        def _():
+            halo(0, tile + 1).start()
+
+        @pl.when(tile > 0)
+        def _():
+            halo(1, tile - 1).start()
+
+        for j in range(4):
+            @pl.when(wanted(tile, j))
             def _():
                 copies, here = own_copies(j)
                 for copy in copies:
                     copy.start()
                 here.start()
 
+        @pl.when(tile > 0)
+        def _():
+            halo(0, tile - 1).wait_recv()
+
+        @pl.when(tile == 0)
+        def _():
+            halo_ref[0] = jnp.zeros(halo_ref.shape[1:], halo_ref.dtype)
+
+        @pl.when(tile < ends)
+        def _():
+            halo(1, tile + 1).wait_recv()
+
+        @pl.when(tile == ends)
+        def _():
+            halo_ref[1] = jnp.zeros(halo_ref.shape[1:], halo_ref.dtype)
+
     for d, when in ((1, 4), (3, 5), (2, 6)):
         @pl.when(step == when)
         def _():
-            for j in range(3):
-                unit, onward = passed_on(d, j)
-
-                @pl.when(wanted(unit))
+            for j in range(4):
+                owner, onward = passed_on(d, j)
+
+                @pl.when(wanted(owner, j))
                 def _():
-                    remote(attend_ref.at[:, j * HD:(j + 1) * HD], unit, d, j, beside).wait_recv()
+                    remote(source(j), owner, d, j, beside).wait_recv()
                     onward.start()
 
     @pl.when(step == last)
     def _():
-        for j in range(3):
-            @pl.when(wanted(tile * 3 + j))
+        @pl.when(tile < ends)
+        def _():
+            halo(0, tile + 1).wait_send()
+
+        @pl.when(tile > 0)
+        def _():
+            halo(1, tile - 1).wait_send()
+
+        for j in range(4):
+            @pl.when(wanted(tile, j))
             def _():
                 copies, here = own_copies(j)
                 for copy in copies:
@@ -152,31 +209,31 @@
                 here.wait()
 
             for d in (1, 2, 3):
-                unit, onward = passed_on(d, j)
-
-                @pl.when(wanted(unit))
+                owner, onward = passed_on(d, j)
+
+                @pl.when(wanted(owner, j))
                 def _():
                     onward.wait_send()
 
             for kind, back in ((0, 0), (4, 1), (5, 2), (6, 3)):
-                unit = (((row - back) % 4) * 2 + 1 - col) * 3 + j
-
-                @pl.when(wanted(unit))
+                owner = ((row - back) % 4) * 2 + 1 - col
+
+                @pl.when(wanted(owner, j))
                 def _():
-                    remote(attend_ref.at[:, j * HD:(j + 1) * HD], unit, kind, j, beside).wait_recv()
+                    remote(source(j), owner, kind, j, beside).wait_recv()
 
 
 def encode_kernel(share, *refs):
     vol_ref, t1_ref, taps_ref, code_ref, mask_ref, emb_ref, w_ref = refs[:7]
     if share:
-        attend_ref, tok_ref, norm_ref, own_ref = refs[7:11]
-        win_ref, maps_ref, acc_ref, t2_ref = refs[11:15]
+        attend_ref, mixing_ref, tok_ref, norm_ref, own_ref, mix_ref = refs[7:13]
+        win_ref, maps_ref, acc_ref, t2_ref, halo_ref = refs[13:18]
     else:
         tok_ref, norm_ref, win_ref, maps_ref, acc_ref, t2_ref = refs[7:]
     step = pl.program_id(0)
     last = pl.num_programs(0) - 1
     if share:
-        share_steps(step, last, attend_ref, own_ref, *refs[15:])
+        share_steps(step, last, vol_ref, attend_ref, mixing_ref, own_ref, mix_ref, halo_ref, *refs[18:])
 
     @pl.when(step == 0)
     def _():
@@ -197,9 +254,8 @@
         down_ok = (row < 2) & (lane % 16 <= 14)
         zc = lax.broadcasted_iota(jnp.int32, (16, 128), 1) // 16 % 2
 
-        @pl.loop(0, vol_ref.shape[0])
-        def _(x):
-            here = vol_ref[x].astype(jnp.float32)
+        def window_plane(x, plane):
+            here = plane.astype(jnp.float32)
             below = jnp.where(zc == 1, pltpu.roll(here[48:], 16, 1), 0.0)
             above = jnp.where(zc == 0, pltpu.roll(here[:16], 112, 1), 0.0)
             planes = jnp.concatenate([below, here, above], axis=0)
@@ -209,6 +265,16 @@
                 win_ref[x, 24 * q:24 * q + 16] = planes[16 * q:16 * q + 16]
                 win_ref[x, 24 * q + 16:24 * q + 24] = halo[16 * q:16 * q + 8] + pltpu.roll(
                     halo[16 * q + 8:16 * q + 16], 4, 0)
+
+        @pl.loop(0, vol_ref.shape[0])
+        def _(x):
+            window_plane(x + (2 if share else 0), vol_ref[x])
+
+        if share:
+            @pl.loop(0, 2)
+            def _(x):
+                window_plane(x, halo_ref[0, x])
+                window_plane(vol_ref.shape[0] + 2 + x, halo_ref[1, x])
 
     slot = step % 3
     parts = []
@@ -256,9 +322,9 @@
         norm_ref[...] = (wide * scale).astype(jnp.bfloat16)
 
 
-def encode(volume_rows, t1, taps, emb, patch_weight, attend_weight):
-    planes = volume_rows.shape[0]
-    share = attend_weight is not None
+def encode(volume_rows, t1, taps, emb, patch_weight, shared):
+    share = shared is not None
+    planes = volume_rows.shape[0] + (4 if share else 0)
     whole = lambda shape: pl.BlockSpec(shape, lambda s: (0,) * len(shape))
     weight = patch_weight.reshape(CH, 8, 4, 16, D)
     code, mask = jnp.asarray(second_code()), jnp.asarray(edge_mask(), jnp.bfloat16)
@@ -276,12 +342,14 @@
     operands = held + [weight]
     extra = {}
     if share:
-        operands.append(attend_weight)
-        in_specs.append(pl.BlockSpec(memory_space=pl.ANY))
-        out_specs.append(pl.BlockSpec(memory_space=pl.ANY))
-        out_shape.append(jax.ShapeDtypeStruct((D, 768), jnp.bfloat16))
-        scratch += [pltpu.SemaphoreType.DMA((3,)), pltpu.SemaphoreType.DMA((7, 3)),
-                    pltpu.SemaphoreType.DMA((7, 3))]
+        operands += shared
+        in_specs += [pl.BlockSpec(memory_space=pl.ANY)] * 2
+        out_specs += [pl.BlockSpec(memory_space=pl.ANY)] * 2
+        out_shape += [jax.ShapeDtypeStruct((6, D, HD), jnp.bfloat16),
+                      jax.ShapeDtypeStruct((8, 256, HD), jnp.bfloat16)]
+        scratch += [pltpu.VMEM((2, 2, 64, 128), jnp.bfloat16)]
+        scratch += [pltpu.SemaphoreType.DMA((2,))] * 2 + [pltpu.SemaphoreType.DMA((4,))]
+        scratch += [pltpu.SemaphoreType.DMA((7, 4))] * 2
         extra = dict(collective_id=1, has_side_effects=True)
     return pl.pallas_call(
         functools.partial(encode_kernel, share),
@@ -297,10 +365,6 @@
     )(*operands)
 
 
-def settle(values_in):
-    return values_in * lax.rsqrt(jnp.mean(values_in * values_in, axis=-1, keepdims=True) + 1e-05)
-
-
 def embed_time(frame_index):
     frequency = jnp.exp(-math.log(1000.0) * jnp.arange(D, dtype=jnp.float32) / D)
     phase_shift = (jnp.arange(D) % 2).astype(jnp.float32) * (math.pi / 2)
@@ -324,38 +388,56 @@
     return me, (sibling, (me + 2) % 4, (sibling + 2) % 4)
 
 
-def attend_kernel(norm_ref, w_ref, out_ref, rows_ref, qkv_ref, att_ref,
-                  back_ref, send_sem, recv_sem, send_back, recv_back):
+def attend_kernel(norm_ref, w_ref, mix_ref, tok_ref, read_ref, out_ref, rows_ref, qkv_ref, att_ref,
+                  part_ref, back_ref, send_sem, recv_sem, send_back, recv_back):
     me, others = partners()
+    sibling, mirror, diagonal = others
     barrier = pltpu.get_barrier_semaphore()
     for other in others:
         pl.semaphore_signal(barrier, inc=1, device_id={"tm": other},
                             device_id_type=pl.DeviceIdType.MESH)
     pl.semaphore_wait(barrier, 3)
-    sends = [
-        pltpu.make_async_remote_copy(
-            src_ref=norm_ref, dst_ref=rows_ref.at[me], send_sem=send_sem.at[i],
-            recv_sem=recv_sem.at[i], device_id={"tm": other},
+
+    def rows_copy(src, owner, i, target):
+        return pltpu.make_async_remote_copy(
+            src_ref=src, dst_ref=rows_ref.at[owner], send_sem=send_sem.at[i],
+            recv_sem=recv_sem.at[i], device_id={"tm": target},
             device_id_type=pl.DeviceIdType.MESH)
-        for i, other in enumerate(others)
-    ]
-    for send in sends:
-        send.start()
+
+    to_mirror = rows_copy(norm_ref, me, 1, mirror)
+    to_sibling = rows_copy(norm_ref, me, 0, sibling)
+    pass_on = rows_copy(rows_ref.at[mirror], mirror, 2, sibling)
+    to_mirror.start()
+    to_sibling.start()
 
     def project(block, source):
-        total = jnp.dot(source[...], w_ref[...], preferred_element_type=jnp.float32)
-        qkv_ref[block] = total.astype(jnp.bfloat16)
+        rows = source[...]
+        for j in range(3):
+            pair = jnp.concatenate([w_ref[2 * j], w_ref[2 * j + 1]], axis=1)
+            total = jnp.dot(rows, pair, preferred_element_type=jnp.float32)
+            qkv_ref[block, :, 256 * j:256 * j + 256] = total.astype(jnp.bfloat16)
 
     project(me, norm_ref)
-    for i, other in enumerate(others):
-        sends[i].wait_recv()
-        project(other, rows_ref.at[other])
-
-    for head in range(2):
-        lo = head * HD
-        for block in range(4):
+    to_sibling.wait_recv()
+    project(sibling, rows_ref.at[sibling])
+    to_mirror.wait_recv()
+    pass_on.start()
+    project(mirror, rows_ref.at[mirror])
+    pass_on.wait_recv()
+    project(diagonal, rows_ref.at[diagonal])
+
+    def back_copy(block, sender, target):
+        return pltpu.make_async_remote_copy(
+            src_ref=part_ref.at[block], dst_ref=back_ref.at[sender], send_sem=send_back.at[block],
+            recv_sem=recv_back.at[sender], device_id={"tm": target},
+            device_id_type=pl.DeviceIdType.MESH)
+
+    mixing = jnp.concatenate([mix_ref[i] for i in range(mix_ref.shape[0])], axis=1)
+    for block in (3, 0, 2, 1):
+        count = 128 * (block + 1)
+        for head in range(2):
+            lo = head * HD
             query = qkv_ref[block, :, lo:lo + HD]
-            count = 128 * (block + 1)
             keys = qkv_ref[:block + 1, :, 256 + lo:256 + lo + HD].reshape(count, HD)
             values = qkv_ref[:block + 1, :, 512 + lo:512 + lo + HD].reshape(count, HD)
             scores = lax.dot_general(query, keys, (((1,), (1,)), ((), ())),
@@ -368,44 +450,51 @@
             weights = (shifted * inverse).astype(jnp.bfloat16)
             att_ref[block, :, lo:lo + HD] = jnp.dot(
                 weights, values, preferred_element_type=jnp.float32).astype(jnp.bfloat16)
-
-    backs = [
-        pltpu.make_async_remote_copy(
-            src_ref=att_ref.at[other], dst_ref=back_ref.at[me], send_sem=send_back.at[i],
-            recv_sem=recv_back.at[i], device_id={"tm": other},
-            device_id_type=pl.DeviceIdType.MESH)
-        for i, other in enumerate(others)
-    ]
-    for back in backs:
-        back.start()
-    out_ref[:, pl.ds(pl.multiple_of(me * 256, 256), 256)] = att_ref[me]
-    for i, other in enumerate(others):
-        backs[i].wait_recv()
-        out_ref[:, pl.ds(pl.multiple_of(other * 256, 256), 256)] = back_ref[other]
-    for i in range(3):
-        sends[i].wait_send()
-        backs[i].wait_send()
-
-
-def attend(normed, weights):
+        part_ref[block] = jnp.dot(att_ref[block], mixing,
+                                  preferred_element_type=jnp.float32).astype(jnp.bfloat16)
+
+        @pl.when(me != block)
+        def _():
+            back_copy(block, me, block).start()
+
+    residual = tok_ref[...].astype(jnp.float32) + jnp.dot(
+        att_ref[me], mixing, preferred_element_type=jnp.float32)
+    for other in others:
+        back_copy(other, other, other).wait_recv()
+        residual += back_ref[other].astype(jnp.float32)
+    scale = lax.rsqrt(jnp.mean(residual * residual, axis=-1, keepdims=True) + 1e-05)
+    out_ref[...] = jnp.dot((residual * scale).astype(jnp.bfloat16), read_ref[...],
+                           preferred_element_type=jnp.float32).astype(jnp.bfloat16)
+    for copy in (to_sibling, to_mirror, pass_on):
+        copy.wait_send()
+    for other in others:
+        back_copy(other, me, other).wait_send()
+
+
+def attend(normed, weights, mixing, token_rows, projector):
     vmem = pl.BlockSpec(memory_space=pltpu.VMEM)
     return pl.pallas_call(
         attend_kernel,
-        in_specs=[vmem] * 2,
+        in_specs=[vmem] * 5,
         out_specs=vmem,
-        out_shape=jax.ShapeDtypeStruct((128, D), jnp.bfloat16),
+        out_shape=jax.ShapeDtypeStruct((128, projector.shape[1]), jnp.bfloat16),
         scratch_shapes=[
             pltpu.VMEM((4, 128, D), jnp.bfloat16),
             pltpu.VMEM((4, 128, 768), jnp.bfloat16),
             pltpu.VMEM((4, 128, 256), jnp.bfloat16),
-            pltpu.VMEM((4, 128, 256), jnp.bfloat16),
-        ] + [pltpu.SemaphoreType.DMA((3,))] * 4,
+            pltpu.VMEM((4, 128, D), jnp.bfloat16),
+            pltpu.VMEM((4, 128, D), jnp.bfloat16),
+            pltpu.SemaphoreType.DMA((3,)),
+            pltpu.SemaphoreType.DMA((3,)),
+            pltpu.SemaphoreType.DMA((4,)),
+            pltpu.SemaphoreType.DMA((4,)),
+        ],
         compiler_params=pltpu.CompilerParams(collective_id=0, has_side_effects=True,
                                              vmem_limit_bytes=32 * 2**20),
-        cost_estimate=pl.CostEstimate(flops=10**9, bytes_accessed=2 * 2**20,
+        cost_estimate=pl.CostEstimate(flops=10**9, bytes_accessed=4 * 2**20,
                                       transcendentals=4 * 10**5),
         name="attend",
-    )(normed, weights)
+    )(normed, weights, mixing, token_rows, projector)
 
 
 def head_weights(attend_weight):
@@ -424,7 +513,13 @@
     for i, other in enumerate(others):
         piece = lax.ppermute(columns(other), "tm", [(m, m ^ (i + 1)) for m in range(4)])
         weights = lax.dynamic_update_slice_in_dim(weights, piece, other * 256, axis=0)
-    return weights
+    return weights.reshape(D, 6, HD).transpose(1, 0, 2)
+
+
+def head_mixing(mixing_weight):
+    rows = lax.dynamic_slice_in_dim(mixing_weight, lax.axis_index("tm") * 256, 256, axis=0)
+    rows = lax.all_gather(rows, "tile", axis=1, tiled=True)
+    return rows.reshape(256, 8, HD).transpose(1, 0, 2)
 
 
 def local(volume, frame_index, tile_offset, conv_first, conv_second, patch_weight,
@@ -434,27 +529,21 @@
     tiles = lax.axis_size("tile")
     rows = volume.reshape(frames, width, depth // 8, 8, height // 8, 8)
     rows = rows.transpose(1, 3, 5, 0, 2, 4).reshape(width, 64, 128)
-    from_left = lax.ppermute(rows[-2:], "tile", [(i, i + 1) for i in range(tiles - 1)])
-    from_right = lax.ppermute(rows[:2], "tile", [(i + 1, i) for i in range(tiles - 1)])
-    volume_rows = jnp.concatenate([from_left, rows, from_right], axis=0)
-
     time_emb, frequency = embed_time(frame_index)
     space_emb = embed_space(tile_offset, tile_place + jnp.arange(1), jnp.arange(depth // EDGE),
                             jnp.arange(height // EDGE), frequency)
     emb = (time_emb[:, None, :] + space_emb[None]).reshape(-1, D)
     t1, taps = first_band(conv_first), second_taps(conv_second)
     if tiles == 8 and attend_weight.shape[1] == 3 * HD:
-        token_rows, normed, weights = encode(volume_rows, t1, taps, emb, patch_weight, attend_weight)
+        token_rows, normed, weights, mixing = encode(
+            rows, t1, taps, emb, patch_weight, [attend_weight, mixing_weight])
     else:
-        token_rows, normed = encode(volume_rows, t1, taps, emb, patch_weight, None)
-        weights = head_weights(attend_weight)
-    attended_rows = attend(normed, weights)
-    mixed_terms = jnp.dot(attended_rows, lax.all_gather(mixing_weight, "tile", axis=1, tiled=True),
-                          preferred_element_type=jnp.float32)
-    residual = token_rows.astype(jnp.float32) + mixed_terms
-    final_rows = settle(residual).astype(jnp.bfloat16)
-    prediction = jnp.dot(final_rows, cube_output_projector,
-                         preferred_element_type=jnp.float32).astype(jnp.bfloat16)
+        from_left = lax.ppermute(rows[-2:], "tile", [(i, i + 1) for i in range(tiles - 1)])
+        from_right = lax.ppermute(rows[:2], "tile", [(i + 1, i) for i in range(tiles - 1)])
+        rows = jnp.concatenate([from_left, rows, from_right], axis=0)
+        token_rows, normed = encode(rows, t1, taps, emb, patch_weight, None)
+        weights, mixing = head_weights(attend_weight), head_mixing(mixing_weight)
+    prediction = attend(normed, weights, mixing, token_rows, cube_output_projector)
     return prediction.reshape(frames, width // EDGE, depth // EDGE, height // EDGE, -1)
 
 

time: 124 us -> 89.3 us (0.72)
  the two profiles are of different devices: /device:TPU:19 before, /device:TPU:3 now
where the time goes in v4:
time: 89.3 us; the launch traced here: 88.1 us
  Pallas kernels  73.9 us (83%)
  local copies, waits for them, and re-layouts  8.75 us (10%)
  other arithmetic  4.18 us (5%)
  between operations  0.97 us (1%)
    pallas_call x1, Pallas kernels, attend(): pl.pallas_call(attend_kernel, in_specs=[vmem] * 5, out_specs=vmem, out_sh...  37.4 us
    pallas_call x1, Pallas kernels, encode(): pl.pallas_call(functools.partial(encode_kernel, share), grid=(planes - 2,...  36.6 us
    reshape x1, local copies, waits for them, and re-layouts, local(): rows = volume.reshape(frames, width, depth // 8, 8, height // 8, 8)  3.39 us
    transpose x1, local copies, waits for them, and re-layouts, local(): rows = rows.transpose(1, 3, 5, 0, 2, 4).reshape(width, 64, 128)  2.96 us

profile of v4, /device:TPU:3, one launch (start us, length us, event | category | flops | bytes accessed | tf_op | source)
XLA Modules:
  0.0 88.1 jit_solution(16741900886068096151)
XLA Ops:
  0.0 0.0 copy-start
  0.0 0.0 copy-start.8
  0.0 0.0 copy-start.6
  0.0 0.8 convert_multiply_fusion
  0.8 0.3 tile.9
  1.1 0.1 fusion.5
  1.2 1.4 %add_convert_fusion = bf16[3,72,640]{2,1,0:T(8,128)(2,1)S(1)} fusion(f32[3,640]{1,0:T(4,128)S(1)} %get-tuple-element.25, f32[3,640]{1,0:T(4,128)S(1)} %get-tuple-element.26, f32[3,640]{1,0:T(4,128)S(1)} %get-tuple-element.27, f32[3,640]{1,0:T(4,128)S(1)} %get-tuple-element.28, f32[3,640]{1,0:T(4,128)S(1)} %get-tuple-element.29, ...), kind=kLoop, calls=%fused_computation.1 | loop fusion | flops 2488320 | bytes 760320 | tf_op jit(solution)/shard_map/convert
  2.7 0.0 copy-done.8
  2.7 0.6 fusion.6
  4.0 0.7 add_convert_fusion.2
  4.7 0.2 sine_add_fusion
  4.9 0.6 add_convert_fusion.1
  5.4 0.3 add_sine_fusion
  5.8 0.0 copy-done.9
  5.8 0.2 add_sine_fusion.1
  6.0 0.0 copy-done.6
  6.1 3.4 %reshape.269 = bf16[4,8,2,8,16,8]{5,4,3,2,1,0:T(8,128)(2,1)} reshape(bf16[4,8,16,128]{3,2,1,0:T(8,128)(2,1)S(1)} %copy-done.6) | data formatting | bytes 262144 | tf_op jit(solution)/shard_map/reshape | solution.py:530
  9.5 0.0 copy-start.5
  9.5 3.0 %copy.18 = bf16[8,8,8,4,2,16]{5,4,3,2,1,0:T(2,128)(2,1)S(1)} copy(bf16[8,8,8,4,2,16]{2,5,1,4,0,3:T(8,128)(2,1)} %bitcast.47) | data formatting | bytes 262144 | tf_op jit(solution)/shard_map/transpose | solution.py:531
  12.4 0.7 reshape.270.refs_0_
  13.1 0.0 copy-done
  13.1 0.0 copy-done.7
  13.1 0.3 convolution_bitcast_fusion.refs_2_
  13.4 0.0 copy-done.2
  13.4 0.0 copy-done.3
  13.4 0.0 copy-done.4
  13.4 0.0 copy-done.5
  13.4 0.0 copy-start.1
  13.5 36.6 %encode.1 = (bf16[128,1024]{1,0:T(8,128)(2,1)S(1)}, bf16[128,1024]{1,0:T(8,128)(2,1)S(1)}, bf16[6,1024,128]{2,1,0:T(8,128)(2,1)S(1)}, bf16[8,256,128]{2,1,0:T(8,128)(2,1)S(1)}) custom-call(bf16[8,64,128]{2,1,0:T(8,128)(2,1)S(1)} %reshape.270.refs_0_, bf16[256,640]{1,0:T(8,128)(2,1)S(1)} %pad.5.refs_1_, f32[27,16,256]{2,1,0:T(8,128)S(1)} %convolution_bitcast_fusion.refs_2_, ...), custom_call_target="tpu_custom_call" | custom-call | flops 8000000000 | bytes 20971520 | tf_op jit(solution)/shard_map/encode/pallas_call | solution.py:354
  50.1 0.0 copy-done.1
  50.1 37.4 %attend.1 = bf16[128,512]{1,0:T(8,128)(2,1)S(1)} custom-call(bf16[128,1024]{1,0:T(8,128)(2,1)S(1)} %get-tuple-element.9.norm_ref, bf16[6,1024,128]{2,1,0:T(8,128)(2,1)S(1)} %get-tuple-element.10.w_ref, bf16[8,256,128]{2,1,0:T(8,128)(2,1)S(1)} %get-tuple-element.11.mix_ref, bf16[128,1024]{1,0:T(8,128)(2,1)S(1)} %get-tuple-element.12.tok_ref, ...), custom_call_target="tpu_custom_call" | custom-call | flops 1000000000 | bytes 4194304 | tf_op jit(solution)/shard_map/attend/pallas_call | solution.py:476
  87.4 0.7 copy.44
  (18 shorter events, 0.2 us)
Async XLA Ops:
  0.0 13.1 %copy-start = (bf16[16,16,3,3,3]{1,0,4,3,2:T(8,128)(2,1)S(1)}, bf16[16,16,3,3,3]{1,0,4,3,2:T(8,128)(2,1)}, u32[]{:S(2)}) copy-start(bf16[16,16,3,3,3]{1,0,4,3,2:T(8,128)(2,1)} %param.17) | copy-start | bytes 41476
  0.0 2.7 %copy-start.8 = (s32[3]{0:T(128)S(1)}, s32[3]{0:T(128)}, u32[]{:S(2)}) copy-start(s32[3]{0:T(128)} %param.15) | copy-start | bytes 40
  0.0 5.8 %copy-start.9 = (s32[4]{0:T(128)S(1)}, s32[4]{0:T(128)}, u32[]{:S(2)}) copy-start(s32[4]{0:T(128)} %param.14) | copy-start | bytes 52
  0.0 6.0 %copy-start.6 = (bf16[4,8,16,128]{3,2,1,0:T(8,128)(2,1)S(1)}, bf16[4,8,16,128]{3,2,1,0:T(8,128)(2,1)}, u32[]{:S(2)}) copy-start(bf16[4,8,16,128]{3,2,1,0:T(8,128)(2,1)} %param.13) | copy-start | bytes 393220
  9.4 3.7 %copy-start.7 = (bf16[16,256,1]{1,0,2:T(8,128)(2,1)S(1)}, bf16[16,256,1]{1,0,2:T(8,128)(2,1)}, u32[]{:S(2)}) copy-start(bf16[16,256,1]{1,0,2:T(8,128)(2,1)} %constant.86) | copy-start | bytes 24580
  9.4 4.0 %copy-start.2 = (bf16[1024,384]{1,0:T(8,128)(2,1)S(1)}, bf16[1024,384]{1,0:T(8,128)(2,1)}, u32[]{:S(2)}) copy-start(bf16[1024,384]{1,0:T(8,128)(2,1)} %refs_7_.1) | copy-start | bytes 2359300
  9.4 4.0 %copy-start.3 = (bf16[1024,128]{1,0:T(8,128)(2,1)S(1)}, bf16[1024,128]{1,0:T(8,128)(2,1)}, u32[]{:S(2)}) copy-start(bf16[1024,128]{1,0:T(8,128)(2,1)} %refs_8_.1) | copy-start | bytes 786436
  9.4 4.0 %copy-start.4 = (bf16[512,128]{1,0:T(8,128)(2,1)S(1)}, bf16[512,128]{1,0:T(8,128)(2,1)}, u32[]{:S(2)}) copy-start(bf16[512,128]{1,0:T(8,128)(2,1)} %constant.74.clone.refs_4_) | copy-start | bytes 393220
  9.5 4.0 %copy-start.5 = (f32[40,1,256]{2,1,0:T(1,128)S(1)}, f32[40,1,256]{2,1,0:T(1,128)}, u32[]{:S(2)}) copy-start(f32[40,1,256]{2,1,0:T(1,128)} %constant.73.clone.refs_3_) | copy-start | bytes 122884
  13.4 36.6 %copy-start.1 = (bf16[1024,512]{1,0:T(8,128)(2,1)S(1)}, bf16[1024,512]{1,0:T(8,128)(2,1)}, u32[]{:S(2)}) copy-start(bf16[1024,512]{1,0:T(8,128)(2,1)} %read_ref.1) | copy-start | bytes 3145732

commit v5 on v4

--- a/solution.py
+++ b/solution.py
@@ -155,13 +155,17 @@
         def _():
             halo(1, tile - 1).start()
 
+        for way, fits in ((3, row >= 0), (0, row < 3), (2, row > 0), (1, row >= 0),
+                          (0, row == 3), (2, row == 0)):
+            for j in range(4):
+                @pl.when(wanted(tile, j) & fits)
+                def _():
+                    own_copies(j)[0][way].start()
+
         for j in range(4):
             @pl.when(wanted(tile, j))
             def _():
-                copies, here = own_copies(j)
-                for copy in copies:
-                    copy.start()
-                here.start()
+                own_copies(j)[1].start()
 
         @pl.when(tile > 0)
         def _():
@@ -179,13 +183,14 @@
         def _():
             halo_ref[1] = jnp.zeros(halo_ref.shape[1:], halo_ref.dtype)
 
-    for d, when in ((1, 4), (3, 5), (2, 6)):
+    for d, when, fits in ((1, 3, row > 0), (3, 4, row < 3), (2, 6, row >= 0), (1, 8, row == 0),
+                          (3, 8, row == 3)):
         @pl.when(step == when)
         def _():
             for j in range(4):
                 owner, onward = passed_on(d, j)
 
-                @pl.when(wanted(owner, j))
+                @pl.when(wanted(owner, j) & fits)
                 def _():
                     remote(source(j), owner, d, j, beside).wait_recv()
                     onward.start()

time: 89.3 us -> 88.5 us (level); the launches traced: 88.1 us -> 88.3 us
    pallas_call x1, Pallas kernels: 36.6 us -> 38.7 us  [encode(): pl.pallas_call(functools.partial(encode_kernel, share), grid=(planes - 2,...]
    pallas_call x1, Pallas kernels: 37.4 us -> 35.4 us  [attend(): pl.pallas_call(attend_kernel, in_specs=[vmem] * 5, out_specs=vmem, out_sh...]
where the time goes in v5:
time: 88.5 us; the launch traced here: 88.3 us
  Pallas kernels  74.1 us (84%)
  local copies, waits for them, and re-layouts  8.75 us (10%)
  other arithmetic  4.18 us (5%)
  between operations  0.97 us (1%)
    pallas_call x1, Pallas kernels, encode(): pl.pallas_call(functools.partial(encode_kernel, share), grid=(planes - 2,...  38.7 us
    pallas_call x1, Pallas kernels, attend(): pl.pallas_call(attend_kernel, in_specs=[vmem] * 5, out_specs=vmem, out_sh...  35.4 us
    reshape x1, local copies, waits for them, and re-layouts, local(): rows = volume.reshape(frames, width, depth // 8, 8, height // 8, 8)  3.39 us
    transpose x1, local copies, waits for them, and re-layouts, local(): rows = rows.transpose(1, 3, 5, 0, 2, 4).reshape(width, 64, 128)  2.96 us

profile of v5, /device:TPU:3, one launch (start us, length us, event | category | flops | bytes accessed | tf_op | source)
XLA Modules:
  0.0 88.3 jit_solution(944340682321421542)
XLA Ops:
  0.0 0.0 copy-start
  0.0 0.0 copy-start.8
  0.0 0.0 copy-start.6
  0.0 0.8 convert_multiply_fusion
  0.8 0.3 tile.9
  1.1 0.1 fusion.5
  1.2 1.4 %add_convert_fusion = bf16[3,72,640]{2,1,0:T(8,128)(2,1)S(1)} fusion(f32[3,640]{1,0:T(4,128)S(1)} %get-tuple-element.25, f32[3,640]{1,0:T(4,128)S(1)} %get-tuple-element.26, f32[3,640]{1,0:T(4,128)S(1)} %get-tuple-element.27, f32[3,640]{1,0:T(4,128)S(1)} %get-tuple-element.28, f32[3,640]{1,0:T(4,128)S(1)} %get-tuple-element.29, ...), kind=kLoop, calls=%fused_computation.1 | loop fusion | flops 2488320 | bytes 760320 | tf_op jit(solution)/shard_map/convert
  2.7 0.0 copy-done.8
  2.7 0.6 fusion.6
  4.0 0.7 add_convert_fusion.2
  4.7 0.2 sine_add_fusion
  4.9 0.6 add_convert_fusion.1
  5.4 0.3 add_sine_fusion
  5.8 0.0 copy-done.9
  5.8 0.2 add_sine_fusion.1
  6.0 0.0 copy-done.6
  6.1 3.4 %reshape.269 = bf16[4,8,2,8,16,8]{5,4,3,2,1,0:T(8,128)(2,1)} reshape(bf16[4,8,16,128]{3,2,1,0:T(8,128)(2,1)S(1)} %copy-done.6) | data formatting | bytes 262144 | tf_op jit(solution)/shard_map/reshape | solution.py:535
  9.5 0.0 copy-start.5
  9.5 3.0 %copy.18 = bf16[8,8,8,4,2,16]{5,4,3,2,1,0:T(2,128)(2,1)S(1)} copy(bf16[8,8,8,4,2,16]{2,5,1,4,0,3:T(8,128)(2,1)} %bitcast.47) | data formatting | bytes 262144 | tf_op jit(solution)/shard_map/transpose | solution.py:536
  12.4 0.7 reshape.270.refs_0_
  13.1 0.0 copy-done
  13.1 0.0 copy-done.7
  13.1 0.3 convolution_bitcast_fusion.refs_2_
  13.4 0.0 copy-done.2
  13.4 0.0 copy-done.3
  13.4 0.0 copy-done.4
  13.4 0.0 copy-done.5
  13.4 0.0 copy-start.1
  13.5 38.7 %encode.1 = (bf16[128,1024]{1,0:T(8,128)(2,1)S(1)}, bf16[128,1024]{1,0:T(8,128)(2,1)S(1)}, bf16[6,1024,128]{2,1,0:T(8,128)(2,1)S(1)}, bf16[8,256,128]{2,1,0:T(8,128)(2,1)S(1)}) custom-call(bf16[8,64,128]{2,1,0:T(8,128)(2,1)S(1)} %reshape.270.refs_0_, bf16[256,640]{1,0:T(8,128)(2,1)S(1)} %pad.5.refs_1_, f32[27,16,256]{2,1,0:T(8,128)S(1)} %convolution_bitcast_fusion.refs_2_, ...), custom_call_target="tpu_custom_call" | custom-call | flops 8000000000 | bytes 20971520 | tf_op jit(solution)/shard_map/encode/pallas_call | solution.py:359
  52.2 0.0 copy-done.1
  52.2 35.4 %attend.1 = bf16[128,512]{1,0:T(8,128)(2,1)S(1)} custom-call(bf16[128,1024]{1,0:T(8,128)(2,1)S(1)} %get-tuple-element.9.norm_ref, bf16[6,1024,128]{2,1,0:T(8,128)(2,1)S(1)} %get-tuple-element.10.w_ref, bf16[8,256,128]{2,1,0:T(8,128)(2,1)S(1)} %get-tuple-element.11.mix_ref, bf16[128,1024]{1,0:T(8,128)(2,1)S(1)} %get-tuple-element.12.tok_ref, ...), custom_call_target="tpu_custom_call" | custom-call | flops 1000000000 | bytes 4194304 | tf_op jit(solution)/shard_map/attend/pallas_call | solution.py:481
  87.6 0.7 copy.44
  (18 shorter events, 0.2 us)
Async XLA Ops:
  0.0 13.1 %copy-start = (bf16[16,16,3,3,3]{1,0,4,3,2:T(8,128)(2,1)S(1)}, bf16[16,16,3,3,3]{1,0,4,3,2:T(8,128)(2,1)}, u32[]{:S(2)}) copy-start(bf16[16,16,3,3,3]{1,0,4,3,2:T(8,128)(2,1)} %param.17) | copy-start | bytes 41476
  0.0 2.7 %copy-start.8 = (s32[3]{0:T(128)S(1)}, s32[3]{0:T(128)}, u32[]{:S(2)}) copy-start(s32[3]{0:T(128)} %param.15) | copy-start | bytes 40
  0.0 5.8 %copy-start.9 = (s32[4]{0:T(128)S(1)}, s32[4]{0:T(128)}, u32[]{:S(2)}) copy-start(s32[4]{0:T(128)} %param.14) | copy-start | bytes 52
  0.0 6.0 %copy-start.6 = (bf16[4,8,16,128]{3,2,1,0:T(8,128)(2,1)S(1)}, bf16[4,8,16,128]{3,2,1,0:T(8,128)(2,1)}, u32[]{:S(2)}) copy-start(bf16[4,8,16,128]{3,2,1,0:T(8,128)(2,1)} %param.13) | copy-start | bytes 393220
  9.4 3.7 %copy-start.7 = (bf16[16,256,1]{1,0,2:T(8,128)(2,1)S(1)}, bf16[16,256,1]{1,0,2:T(8,128)(2,1)}, u32[]{:S(2)}) copy-start(bf16[16,256,1]{1,0,2:T(8,128)(2,1)} %constant.86) | copy-start | bytes 24580
  9.4 4.0 %copy-start.2 = (bf16[1024,384]{1,0:T(8,128)(2,1)S(1)}, bf16[1024,384]{1,0:T(8,128)(2,1)}, u32[]{:S(2)}) copy-start(bf16[1024,384]{1,0:T(8,128)(2,1)} %refs_7_.1) | copy-start | bytes 2359300
  9.4 4.0 %copy-start.3 = (bf16[1024,128]{1,0:T(8,128)(2,1)S(1)}, bf16[1024,128]{1,0:T(8,128)(2,1)}, u32[]{:S(2)}) copy-start(bf16[1024,128]{1,0:T(8,128)(2,1)} %refs_8_.1) | copy-start | bytes 786436
  9.4 4.0 %copy-start.4 = (bf16[512,128]{1,0:T(8,128)(2,1)S(1)}, bf16[512,128]{1,0:T(8,128)(2,1)}, u32[]{:S(2)}) copy-start(bf16[512,128]{1,0:T(8,128)(2,1)} %constant.74.clone.refs_4_) | copy-start | bytes 393220
  9.5 4.0 %copy-start.5 = (f32[40,1,256]{2,1,0:T(1,128)S(1)}, f32[40,1,256]{2,1,0:T(1,128)}, u32[]{:S(2)}) copy-start(f32[40,1,256]{2,1,0:T(1,128)} %constant.73.clone.refs_3_) | copy-start | bytes 122884
  13.4 38.8 %copy-start.1 = (bf16[1024,512]{1,0:T(8,128)(2,1)S(1)}, bf16[1024,512]{1,0:T(8,128)(2,1)}, u32[]{:S(2)}) copy-start(bf16[1024,512]{1,0:T(8,128)(2,1)} %read_ref.1) | copy-start | bytes 3145732
